TPU v7x, 128 devices: a whole 4x4x4 slice. The times are simulated.
128 devices in a mesh: row: 16 (over x, y_hi, core), col: 8 (over y_lo, z).
Axes of the slice: x: 4, y: 4 (y_hi: 2, y_lo: 2; y = y_hi * 2 + y_lo), z: 4, core: 2. Of those that a mesh axis runs over, the one named last changes fastest.
Arguments:
- z_rows: bfloat16 [16, 2048, 128], P('row', 'col'), may hold values from -6 to 6
- z_cols: bfloat16 [16, 2048, 128], P('row', 'col'), may hold values from -6 to 6
- bias_start: bfloat16 [4, 2048, 2048], P(None, 'row', 'col'), may hold values from -6 to 325, as said below
- bias_end: bfloat16 [4, 2048, 2048], P(None, 'row', 'col'), may hold values from -6 to 325, as said below
- w_start_in: bfloat16 [128, 512], replicated, may hold values from -0.5 to 0.5
- w_start_out: bfloat16 [128, 128], replicated, may hold values from -2 to 2
- w_end_in: bfloat16 [128, 512], replicated, may hold values from -0.5 to 0.5
- w_end_out: bfloat16 [128, 128], replicated, may hold values from -2 to 2
- token_mask: int32 [2048], replicated, may hold values 0 or 1
- offsets: int32 [2], replicated, may hold values from 0 to 2032
Outputs:
- out_start: bfloat16 [16, 2048, 128], P('col', 'row')
- out_end: bfloat16 [16, 2048, 128], P('row', 'col')
Inputs may be any that keep to these rules, and one draw needn't show every extreme that they name: `bias_start`: entry [h, j, k] belongs to the pair (j, k). `bias_end`: entry [h, k, i] belongs to the pair (k, i).
All inputs are finite; a program needn't handle non-finite values.
Results may differ from a plain program's by a relative error of at most 0.0082.
Values may be sent and summed in bfloat16 or wider, within the bound.
A program may use at most 128 MiB of HBM per device.

v0:
```python
import jax
import jax.numpy as jnp
from jax import lax
from jax.sharding import PartitionSpec as P


def joined(value, axis, combine):
    everything = jax.tree.map(lambda part: lax.all_gather(part, axis), value)
    first = jax.tree.map(lambda part: part[0], everything)

    def step(k, so_far):
        return combine(so_far, jax.tree.map(lambda part: part[k], everything))

    return lax.fori_loop(1, lax.axis_size(axis), step, first)


def normalize(pair_block):
    values = pair_block.astype(jnp.float32)
    center = values - jnp.mean(values, axis=-1, keepdims=True)
    spread = jnp.mean(center * center, axis=-1, keepdims=True)
    return (center * lax.rsqrt(spread + 1e-05)).astype(jnp.bfloat16)


def project(normed, weights, column, factor):
    channels = weights.shape[0]
    chosen = weights[:, column * channels : (column + 1) * channels]
    result = jnp.dot(normed.reshape(-1, channels), chosen, preferred_element_type=jnp.float32)
    return result.reshape(normed.shape[:-1] + (channels,)) * factor


def split_heads(array, head_count):
    return array.reshape(array.shape[:-1] + (head_count, array.shape[-1] // head_count))


def spread_heads(totals, factors):
    row_count, span_count, channels = totals.shape
    head_count = factors.shape[1]
    shaped = totals.reshape(row_count, span_count, head_count, channels // head_count)
    shaped = shaped * jnp.transpose(factors, (0, 2, 1))[..., None]
    return shaped.reshape(row_count, span_count, channels)


def divide_heads(totals, denominator):
    row_count, span_count, channels = totals.shape
    head_count = denominator.shape[1]
    shaped = totals.reshape(row_count, span_count, head_count, channels // head_count)
    shaped = shaped / jnp.transpose(denominator, (0, 2, 1))[..., None]
    return shaped.reshape(row_count, span_count, channels)


def combine_parts(earlier, later_parts):
    largest = jnp.maximum(earlier[0], later_parts[0])
    early_factor = jnp.exp(earlier[0] - largest)
    late_factor = jnp.exp(later_parts[0] - largest)
    summed = spread_heads(earlier[1], early_factor) + spread_heads(later_parts[1], late_factor)
    return (largest, summed, earlier[2] * early_factor + later_parts[2] * late_factor)


def start_block(block_items, bias_tile, key_bias):
    query_rows, key_rows, value_rows = block_items
    scores = jnp.einsum("abhd,akhd->ahbk", query_rows, key_rows, preferred_element_type=jnp.float32)
    scores = scores + bias_tile + key_bias
    maxima = jnp.max(scores, axis=-1)
    exponent = jnp.exp(scores - maxima[..., None])
    totals = jnp.sum(exponent, axis=-1)
    numerator = jnp.einsum(
        "ahbk,akhd->abhd",
        exponent.astype(jnp.bfloat16),
        value_rows,
        preferred_element_type=jnp.float32,
    )
    return (maxima, numerator.reshape(numerator.shape[0], numerator.shape[1], -1), totals)


def end_block(block_items, bias_tile, key_bias):
    query_rows, key_rows, value_rows = block_items
    scores = jnp.einsum("akhd,abhd->ahkb", key_rows, query_rows, preferred_element_type=jnp.float32)
    scores = scores + bias_tile + key_bias[:, None]
    maxima = jnp.max(scores, axis=2)
    exponent = jnp.exp(scores - maxima[:, :, None, :])
    totals = jnp.sum(exponent, axis=2)
    numerator = jnp.einsum(
        "ahkb,akhd->abhd",
        exponent.astype(jnp.bfloat16),
        value_rows,
        preferred_element_type=jnp.float32,
    )
    return (maxima, numerator.reshape(numerator.shape[0], numerator.shape[1], -1), totals)


def run_blocks(block_function, query_rows, key_rows, value_rows, bias_tile, key_bias):
    stacked = tuple(
        (
            member.reshape((member.shape[0] // 2, 2) + member.shape[1:])
            for member in (query_rows, key_rows, value_rows)
        )
    )
    maxima, numerator, totals = lax.map(
        lambda block_items: block_function(block_items, bias_tile, key_bias), stacked
    )
    maxima = maxima.reshape((-1,) + maxima.shape[2:])
    numerator = numerator.reshape((-1,) + numerator.shape[2:])
    totals = totals.reshape((-1,) + totals.shape[2:])
    return (maxima, numerator, totals)


def finish(attended, gate_values, out_weight, row_mask, column_mask):
    gated_rows = (jax.nn.sigmoid(gate_values) * attended).astype(jnp.bfloat16)
    channels = gated_rows.shape[-1]
    result = jnp.dot(
        gated_rows.reshape(-1, channels), out_weight, preferred_element_type=jnp.float32
    )
    result = result.reshape(gated_rows.shape)
    return (result * (row_mask[:, None] * column_mask[None, :])[..., None]).astype(jnp.bfloat16)


def local(
    z_rows,
    z_cols,
    bias_start,
    bias_end,
    w_start_in,
    w_start_out,
    w_end_in,
    w_end_out,
    token_mask,
    offsets,
):
    row_devices = lax.axis_size("row")
    column_devices = lax.axis_size("col")
    row_index = lax.axis_index("row")
    column_index = lax.axis_index("col")
    head_count = bias_start.shape[0]
    tile_width = bias_start.shape[1]
    local_rows, column_span, channels = z_rows.shape
    slab_rows = local_rows * row_devices
    query_scale = (channels // head_count) ** (-0.5)
    normed_start = normalize(z_rows)
    normed_end = normalize(z_cols)
    keys_start = project(normed_start, w_start_in, 1, 1.0).astype(jnp.bfloat16)
    values_start = project(normed_start, w_start_in, 2, 1.0).astype(jnp.bfloat16)
    query_end = project(normed_end, w_end_in, 0, query_scale).astype(jnp.bfloat16)
    keys_start, values_start, query_end = (
        lax.all_gather(keys_start, "row", axis=0, tiled=True),
        lax.all_gather(values_start, "row", axis=0, tiled=True),
        lax.all_gather(query_end, "row", axis=0, tiled=True),
    )
    wide_start, wide_end = (
        lax.all_gather(normed_start, "col", axis=1, tiled=True),
        lax.all_gather(normed_end, "col", axis=1, tiled=True),
    )
    near_start, near_end = (
        lax.all_to_all(wide_start, "row", split_axis=1, concat_axis=0, tiled=True),
        lax.all_to_all(wide_end, "row", split_axis=1, concat_axis=0, tiled=True),
    )
    query_start = project(near_start, w_start_in, 0, query_scale).astype(jnp.bfloat16)
    keys_end = project(near_end, w_end_in, 1, 1.0).astype(jnp.bfloat16)
    values_end = project(near_end, w_end_in, 2, 1.0).astype(jnp.bfloat16)
    mask_float = token_mask.astype(jnp.float32)
    start_key_bias = (
        lax.dynamic_slice_in_dim(mask_float, column_index * column_span, column_span) - 1.0
    ) * 1000000000.0
    end_key_bias = (
        lax.dynamic_slice_in_dim(mask_float, row_index * tile_width, tile_width) - 1.0
    ) * 1000000000.0
    peak_start, numer_start, denom_start = run_blocks(
        start_block,
        split_heads(query_start, head_count),
        split_heads(keys_start, head_count),
        split_heads(values_start, head_count),
        bias_start,
        start_key_bias,
    )
    per_column = slab_rows // column_devices
    first_row = column_index * per_column
    peak_start, numer_start, denom_start = joined(
        (peak_start, numer_start, denom_start), "col", combine_parts
    )
    attend_start = lax.dynamic_slice_in_dim(
        divide_heads(numer_start, denom_start), first_row, per_column, 0
    )
    near_rows = lax.dynamic_slice_in_dim(near_start, first_row, per_column, 0)
    gate_start = project(near_rows, w_start_in, 3, 1.0)
    start_rows_mask = lax.dynamic_slice_in_dim(mask_float, offsets[0] + first_row, per_column)
    start_cols_mask = lax.dynamic_slice_in_dim(mask_float, row_index * tile_width, tile_width)
    out_start = finish(attend_start, gate_start, w_start_out, start_rows_mask, start_cols_mask)
    peak_end, numer_end, denom_end = run_blocks(
        end_block,
        split_heads(query_end, head_count),
        split_heads(keys_end, head_count),
        split_heads(values_end, head_count),
        bias_end,
        end_key_bias,
    )
    first_end = row_index * local_rows
    peak_end, numer_end, denom_end = joined((peak_end, numer_end, denom_end), "row", combine_parts)
    attend_end = lax.dynamic_slice_in_dim(
        divide_heads(numer_end, denom_end), first_end, local_rows, 0
    )
    gate_end = project(normed_end, w_end_in, 3, 1.0)
    end_rows_mask = lax.dynamic_slice_in_dim(mask_float, offsets[1] + first_end, local_rows)
    end_cols_mask = lax.dynamic_slice_in_dim(mask_float, column_index * column_span, column_span)
    out_end = finish(attend_end, gate_end, w_end_out, end_rows_mask, end_cols_mask)
    return (out_start, out_end)


def solution(mesh):
    return jax.shard_map(
        local,
        mesh=mesh,
        in_specs=(
            P("row", "col", None),
            P("row", "col", None),
            P(None, "row", "col"),
            P(None, "row", "col"),
            P(),
            P(),
            P(),
            P(),
            P(),
            P(),
        ),
        out_specs=(P("col", "row", None), P("row", "col", None)),
        check_vma=False,
    )
```

profile of v0, /device:TPU:1, one launch (start us, length us, event | category | flops | bytes accessed | tf_op | source)
XLA Modules:
  0.0 688.2 jit_solution(17558906516407444269)
XLA Ops:
  16.4 26.5 %all_gather.39 = bf16[1,2048,128]{2,1,0:T(8,128)(2,1)S(1)} all-gather(bf16[1,256,128]{2,1,0:T(8,128)(2,1)S(1)} %fusion.55), channel_id=1, replica_groups=mesh['row'=16,'col'=8] {'col'}, dimensions={1}, use_global_device_ids=true | all-gather | bytes 589824 | tf_op jit(solution)/shard_map/all_gather | solution.py:150
  42.9 8.1 %copy.179 = bf16[1,2048,128]{2,0,1:T(2,128)(2,1)S(1)} copy(bf16[1,2048,128]{2,1,0:T(8,128)(2,1)S(1)} %all_gather.39) | data formatting | bytes 1048576 | tf_op jit(solution)/shard_map/all_gather | solution.py:150
  51.5 11.4 %reduce.5 = bf16[2048,128]{1,0:T(8,128)(2,1)S(1)} reduce(bf16[2048,1,128]{2,1,0:T(2,128)(2,1)S(1)} %bitcast.247, bf16[]{:T(256)} %broadcast.149), dimensions={1}, to_apply=%bitcast.197.reduce_sub_computation | reduce | bytes 1048578
  63.9 12.6 %all-to-all-start.1 = ((bf16[16,2,8192]{2,1,0:T(2,128)(2,1)}), bf16[16,2,8192]{2,1,0:T(2,128)(2,1)S(1)}, u32[]{:S(2)}, u32[]{:S(2)}) async-start(bf16[16,2,8192]{2,1,0:T(2,128)(2,1)} %reshape.235), calls=%async_computation.1 | async-start | bytes 1048576 | tf_op jit(solution)/shard_map/all_to_all | solution.py:154
  78.4 9.4 %all-to-all-done.1 = bf16[16,2,8192]{2,1,0:T(2,128)(2,1)S(1)} async-done(((bf16[16,2,8192]{2,1,0:T(2,128)(2,1)}), bf16[16,2,8192]{2,1,0:T(2,128)(2,1)S(1)}, u32[]{:S(2)}, u32[]{:S(2)}) %all-to-all-start.1) | async-done | bytes 524320 | tf_op jit(solution)/shard_map/all_to_all | solution.py:154
  92.3 26.4 %while.68 = (s32[]{:T(128)}, f32[8,2,4,256]{3,2,1,0:T(4,128)}, f32[8,2,256,128]{3,2,1,0:T(8,128)}, f32[8,2,4,256]{3,2,1,0:T(4,128)}, bf16[8,2,128,4,32]{2,4,3,1,...) while((s32[]{:T(128)}, f32[8,2,4,256]{3,2,1,0:T(4,128)}, ...), condition=%wide.region_13.14_spmd, body=%wide.region_10.13_spmd.sunk | while | flops 35516416 | bytes 6359149 | solution.py:98
  120.2 23.3 %all_gather.33 = bf16[1,2048,128]{2,1,0:T(8,128)(2,1)S(1)} all-gather(bf16[1,256,128]{2,1,0:T(8,128)(2,1)S(1)} %fusion.57), channel_id=1, replica_groups=mesh['row'=16,'col'=8] {'col'}, dimensions={1}, use_global_device_ids=true | all-gather | bytes 589824 | tf_op jit(solution)/shard_map/all_gather | solution.py:149
  143.5 8.1 %copy.180 = bf16[1,2048,128]{2,0,1:T(2,128)(2,1)S(1)} copy(bf16[1,2048,128]{2,1,0:T(8,128)(2,1)S(1)} %all_gather.33) | data formatting | bytes 1048576 | tf_op jit(solution)/shard_map/all_gather | solution.py:149
  151.6 11.4 %reduce.4 = bf16[2048,128]{1,0:T(8,128)(2,1)S(1)} reduce(bf16[2048,1,128]{2,1,0:T(2,128)(2,1)S(1)} %bitcast.248, bf16[]{:T(256)} %broadcast.149), dimensions={1}, to_apply=%bitcast.198.reduce_sub_computation | reduce | bytes 1048578
  164.0 10.5 %all-to-all-start = ((bf16[16,2,8192]{2,1,0:T(2,128)(2,1)}), bf16[16,2,8192]{2,1,0:T(2,128)(2,1)S(1)}, u32[]{:S(2)}, u32[]{:S(2)}) async-start(bf16[16,2,8192]{2,1,0:T(2,128)(2,1)} %reshape.233), calls=%async_computation | async-start | bytes 1048576 | tf_op jit(solution)/shard_map/all_to_all | solution.py:153
  177.5 8.1 %all-to-all-done = bf16[16,2,8192]{2,1,0:T(2,128)(2,1)S(1)} async-done(((bf16[16,2,8192]{2,1,0:T(2,128)(2,1)}), bf16[16,2,8192]{2,1,0:T(2,128)(2,1)S(1)}, u32[]{:S(2)}, u32[]{:S(2)}) %all-to-all-start) | async-done | bytes 524320 | tf_op jit(solution)/shard_map/all_to_all | solution.py:153
  194.4 25.4 %while.66 = (s32[]{:T(128)}, f32[8,2,4,128]{3,1,0,2:T(2,128)S(1)}, f32[8,2,128,128]{3,2,1,0:T(8,128)}, f32[8,2,4,128]{3,1,0,2:T(2,128)S(1)}, bf16[8,2,128,4,32]{...) while((s32[]{:T(128)}, f32[8,2,4,128]{3,1,0,2:T(2,128)S(1)}, ...), condition=%wide.region_5.6_spmd, body=%wide.region_2.5_spmd.sunk | while | flops 35518464 | bytes 5998197 | solution.py:98
  221.3 24.5 %all_gather.36 = f32[8,16,4,128]{3,1,2,0:T(8,128)} all-gather(f32[1,16,4,128]{3,1,2,0:T(8,128)S(1)} %bitcast.264), channel_id=1, replica_groups=mesh['row'=16,'col'=8] {'col'}, dimensions={0}, use_global_device_ids=true | all-gather | bytes 294912 | tf_op jit(solution)/shard_map/all_gather | solution.py:8
  246.6 26.4 %all_gather.38 = f32[8,16,4,128]{3,1,2,0:T(8,128)} all-gather(f32[1,16,4,128]{3,1,2,0:T(8,128)S(1)} %bitcast.265), channel_id=1, replica_groups=mesh['row'=16,'col'=8] {'col'}, dimensions={0}, use_global_device_ids=true | all-gather | bytes 294912 | tf_op jit(solution)/shard_map/all_gather | solution.py:8
  275.7 66.0 %all-gather.11.cloned.1.call-done = f32[8,16,128,128]{3,2,1,0:T(8,128)} async-done(((f32[1,16,128,128]{3,2,1,0:T(8,128)}), f32[8,16,128,128]{3,2,1,0:T(8,128)}) %all-gather.11.cloned.1.call-update) | async-done | bytes 8388624 | tf_op jit(solution)/shard_map/all_gather | solution.py:8
  343.4 21.6 %while.67 = (s32[]{:T(128)}, f32[16,4,128]{2,1,0:T(4,128)S(1)}, f32[16,128,128]{1,2,0:T(8,128)S(1)}, f32[16,4,128]{2,1,0:T(4,128)S(1)}, f32[8,16,4,128]{3,1,2,0:...) while((s32[]{:T(128)}, f32[16,4,128]{2,1,0:T(4,128)S(1)}, ...), condition=%wide.region_7.8_spmd, body=%wide.region_6.7_spmd.sunk | while | flops 851973 | bytes 7962775 | solution.py:14
  367.3 163.4 %all-gather.15.cloned.1.call-done = f32[16,16,256,128]{3,2,1,0:T(8,128)} async-done(((f32[1,16,256,128]{3,2,1,0:T(8,128)}), f32[16,16,256,128]{3,2,1,0:T(8,128)}) %all-gather.15.cloned.1.call-update) | async-done | bytes 33554448 | tf_op jit(solution)/shard_map/all_gather | solution.py:8
  534.2 141.9 %while.69 = (s32[]{:T(128)}, f32[16,4,256]{2,1,0:T(4,128)S(1)}, f32[16,256,128]{1,2,0:T(8,128)}, f32[16,4,256]{2,1,0:T(4,128)S(1)}, f32[16,16,4,256]{3,1,2,0:T(8...) while((s32[]{:T(128)}, f32[16,4,256]{2,1,0:T(4,128)S(1)}, ...), condition=%wide.region_15.16_spmd, body=%wide.region_14.15_spmd.sunk | while | flops 1703941 | bytes 15925399 | solution.py:14
  540.4 3.2 fusion.128
  549.9 3.2 fusion.128
  559.4 3.2 fusion.128
  568.8 3.2 fusion.128
  578.3 3.2 fusion.128
  587.7 3.2 fusion.128
  597.2 3.2 fusion.128
  606.6 3.2 fusion.128
  616.1 3.2 fusion.128
  625.6 3.2 fusion.128
  635.0 3.2 fusion.128
  644.5 3.2 fusion.128
  653.9 3.2 fusion.128
  663.4 3.2 fusion.128
  (385 shorter events, 215.9 us)
Async XLA Ops:
  7.2 358.3 %copy-start = (bf16[128,128]{1,0:T(8,128)(2,1)S(1)}, bf16[128,128]{1,0:T(8,128)(2,1)}, u32[]{:S(2)}) copy-start(bf16[128,128]{1,0:T(8,128)(2,1)} %param.23) | copy-start | bytes 98308
  7.2 82.8 %all-gather.23.cloned.1.call-start = ((), (), s32[]{:S(2)}) async-start(), calls=%async_computation.8 | async-start | bytes 1114112 | tf_op jit(solution)/shard_map/all_gather | solution.py:146
  10.2 6.2 copy-start.5
  11.8 177.0 %all-gather.19.cloned.1.call-start = ((), (), s32[]{:S(2)}) async-start(), calls=%async_computation.6 | async-start | bytes 1114112 | tf_op jit(solution)/shard_map/all_gather | solution.py:144
  51.0 27.4 %copy-start.9 = (s32[2048]{0:T(1024)S(1)}, s32[2048]{0:T(1024)}, u32[]{:S(2)}) copy-start(s32[2048]{0:T(1024)} %param.26) | copy-start | bytes 24580
  63.9 24.6 %copy-start.7 = (bf16[128,512]{1,0:T(8,128)(2,1)S(1)}, bf16[128,512]{1,0:T(8,128)(2,1)}, u32[]{:S(2)}) copy-start(bf16[128,512]{1,0:T(8,128)(2,1)} %param.24) | copy-start | bytes 393220
  63.9 23.9 %all-to-all-start.1 = ((bf16[16,2,8192]{2,1,0:T(2,128)(2,1)}), bf16[16,2,8192]{2,1,0:T(2,128)(2,1)S(1)}, u32[]{:S(2)}, u32[]{:S(2)}) async-start(bf16[16,2,8192]{2,1,0:T(2,128)(2,1)} %reshape.235), calls=%async_computation.1 | async-start | bytes 1048576 | tf_op jit(solution)/shard_map/all_to_all | solution.py:154
  76.5 114.7 %all-gather.21.cloned.1.call-start = ((), (), s32[]{:S(2)}) async-start(), calls=%async_computation.7 | async-start | bytes 1114112 | tf_op jit(solution)/shard_map/all_gather | solution.py:145
  78.1 195.8 %all-gather.13.cloned.1.call-start = ((), (), s32[]{:S(2)}) async-start(), calls=%async_computation.3 | async-start | bytes 1114112 | tf_op jit(solution)/shard_map/all_gather | solution.py:8
  89.9 2.3 copy-start.2
  151.6 23.2 %copy-start.10 = (s32[2]{0:T(128)S(1)}, s32[2]{0:T(128)}, u32[]{:S(2)}) copy-start(s32[2]{0:T(128)} %param.27) | copy-start | bytes 28
  164.0 21.7 %all-to-all-start = ((bf16[16,2,8192]{2,1,0:T(2,128)(2,1)}), bf16[16,2,8192]{2,1,0:T(2,128)(2,1)S(1)}, u32[]{:S(2)}, u32[]{:S(2)}) async-start(bf16[16,2,8192]{2,1,0:T(2,128)(2,1)} %reshape.233), calls=%async_computation | async-start | bytes 1048576 | tf_op jit(solution)/shard_map/all_to_all | solution.py:153
  174.5 100.3 %all-gather.17.cloned.1.call-start = ((), (), s32[]{:S(2)}) async-start(), calls=%async_computation.5 | async-start | bytes 1114112 | tf_op jit(solution)/shard_map/all_gather | solution.py:8
  177.5 10.7 %copy-start.8 = (f32[8,2,4,256]{3,2,1,0:T(4,128)S(1)}, f32[8,2,4,256]{3,2,1,0:T(4,128)}, u32[]{:S(2)}) copy-start(f32[8,2,4,256]{3,2,1,0:T(4,128)} %get-tuple-element.461) | copy-start | bytes 196612
  186.3 0.8 copy-start.4
  191.1 3.2 copy-start.3
  194.3 147.4 %all-gather.11.cloned.1.call-start = ((), (), s32[]{:S(2)}) async-start(), calls=%async_computation.2 | async-start | bytes 9437184 | tf_op jit(solution)/shard_map/all_gather | solution.py:8
  219.8 310.9 %all-gather.15.cloned.1.call-start = ((), (), s32[]{:S(2)}) async-start(), calls=%async_computation.4 | async-start | bytes 35651584 | tf_op jit(solution)/shard_map/all_gather | solution.py:8
  676.1 1.6 copy-start.1
  677.7 1.8 copy-start.6
  677.7 1.8 copy-start.11
Sparse Core Ops, SparseCore 0:
  11.9 48.9 all-gather.22
  63.8 44.1 all-gather.18
  111.0 44.3 all-gather.20
  157.6 44.2 all-gather.12
  204.2 43.8 all-gather.16
  249.6 92.0 all-gather.10
  344.1 186.4 all-gather.14
where the time goes:
time: 693 us; the launch traced here: 688 us
  waiting for transfers between devices  248 us (36%)
  local copies, waits for them, and re-layouts  179 us (26%)
  blocking collectives  101 us (15%)
  other arithmetic  90.5 us (13%)
  matrix products  29.3 us (4%)
  starting transfers between devices  23.8 us (3%)
  between operations  16 us (2%)
    all_gather x4, waiting for transfers between devices, joined(): everything = jax.tree.map(lambda part: lax.all_gather(part, axis), value)  229 us
    dynamic_slice x66, local copies, waits for them, and re-layouts, step(): return combine(so_far, jax.tree.map(lambda part: part[k], everything))  107 us
    add x22, other arithmetic, combine_parts(): spread_heads(earlier[1], early_factor)  51.7 us
    all_gather x2, blocking collectives, joined(): everything = jax.tree.map(lambda part: lax.all_gather(part, axis), value)  51 us
    all_gather x1, blocking collectives, local(): lax.all_gather(normed_end, 'col', axis=1, tiled=True)  26.5 us
    all_gather x1, blocking collectives, local(): lax.all_gather(normed_start, 'col', axis=1, tiled=True)  23.3 us
    unnamed x2, other arithmetic  22.9 us
    dynamic_update_slice x48, local copies, waits for them, and re-layouts, run_blocks(): lax.map(lambda block_items: block_function(block_items, bias_tile, key_bi...  18.1 us
  transfers between devices with their start and end apart: 9, of which 4 were waited for; matrix products, arithmetic and copies ran while one was open for 21% of the time, Pallas kernels for 0%

commit v1 on v0

v1 whole, which is shorter than its diff:
```python
import functools
import math

import jax
import jax.numpy as jnp
from jax import lax
from jax.experimental import pallas as pl
from jax.experimental.pallas import tpu as pltpu
from jax.sharding import PartitionSpec as P

MESH = pl.DeviceIdType.MESH
LOG2E = math.log2(math.e)
LOOK = 2
F32 = jnp.float32
BF16 = jnp.bfloat16


def nn(a, b):
    return lax.dot_general(a, b, (((1,), (0,)), ((), ())), preferred_element_type=F32)


def nt(a, b):
    return lax.dot_general(a, b, (((1,), (1,)), ((), ())), preferred_element_type=F32)


def normalize(block):
    values = block.astype(F32)
    center = values - jnp.mean(values, axis=-1, keepdims=True)
    spread = jnp.mean(center * center, axis=-1, keepdims=True)
    return (center * lax.rsqrt(spread + 1e-05)).astype(BF16)


def kernel(
    n, nc, heads,
    zr, zc, bs, be, ws, wso, we, weo, tm, tms, offs,
    out_s, out_e,
    x, kv, q, bias, wvt, wgt, be_in, pn, pst, rsn, rss, ren, res,
    sg, sn, sf, spn, sps, sb,
    rg, rn, rf, rsn_sem, rss_sem, ren_sem, res_sem, rb,
):
    r = lax.axis_index("row")
    c = lax.axis_index("col")
    core = lax.rem(r, 2)
    chip = r // 2
    mate = r + 1 - 2 * core
    tile = tm.shape[1]
    channels = zr.shape[2]
    depth = channels // heads
    per = n // nc
    mine = pl.ds(pl.multiple_of(core * tile, tile), tile)
    other = pl.ds(pl.multiple_of((1 - core) * tile, tile), tile)
    diagonal = chip == c

    def peer(u):
        return lax.rem((r + 1) // 2 + u + nc - c, nc)

    def turn(t):
        return lax.rem(2 * (chip + c) + 2 * n - t, n)

    barrier = pltpu.get_barrier_semaphore()

    def greet(row, col):
        pl.semaphore_signal(barrier, inc=1, device_id=(row, col), device_id_type=MESH)

    def greet_row(d, carry):
        greet(lax.rem(r + d, n), c)
        return carry

    def greet_col(d, carry):
        greet(r, lax.rem(c + d, nc))
        return carry

    lax.fori_loop(1, n, greet_row, 0)
    lax.fori_loop(1, nc, greet_col, 0)

    def greet_near(d, carry):
        row_to, col_to = 2 * c + lax.rem(d, 2), d // 2
        @pl.when(jnp.logical_not((row_to == r) & (col_to == c)))
        def _():
            greet(row_to, col_to)
        @pl.when(jnp.logical_not((d == r) & diagonal))
        def _():
            greet(d, chip)
        return carry

    lax.fori_loop(0, n, greet_near, 0)

    x[0] = normalize(zr[0])
    x[1] = normalize(zc[0])

    pl.semaphore_wait(barrier, n - 1 + nc - 1 + 2 * n - jnp.where(diagonal, 2, 0))

    def half(form, e):
        return x.at[form, pl.ds(e * tile, tile)]

    def gather_copy(form, row_to, e):
        if form == 0:
            dst = kv.at[0, r, pl.ds(e * tile, tile)]
        else:
            dst = q.at[1, r]
        return half(form, e), dst, sg.at[form, row_to], rg.at[form, r]

    def near_copy(form, col_to, e):
        if form == 0:
            dst = q.at[0, r]
        else:
            dst = kv.at[1, r, pl.ds(e * tile, tile)]
        return half(form, e), dst, sn.at[form, 2 * col_to + e], rn.at[form, r]

    def remote(src, dst, send, recv, row, col):
        return pltpu.make_async_remote_copy(
            src_ref=src, dst_ref=dst, send_sem=send, recv_sem=recv,
            device_id=(row, col), device_id_type=MESH,
        )

    def either(here, src, dst, send, recv, row, col):
        @pl.when(here)
        def _():
            pltpu.make_async_copy(src, dst, recv).start()
        @pl.when(jnp.logical_not(here))
        def _():
            remote(src, dst, send, recv, row, col).start()

    def sent(here, src, dst, send, recv):
        @pl.when(jnp.logical_not(here))
        def _():
            remote(src, dst, send, recv, mate, c).wait_send()

    bias_swap = remote(
        be.at[:, :, pl.ds(pl.multiple_of((1 - core) * tile, tile), tile)], be_in, sb, rb, mate, c
    )

    def send_form(form):
        def step(u, carry):
            to = peer(u)
            for e in range(2):
                either(2 * to + e == r, *gather_copy(form, 2 * to + e, e), 2 * to + e, c)
                here = (2 * c + e == r) & (to == c)
                either(here, *near_copy(form, to, e), 2 * c + e, to)
            return carry
        lax.fori_loop(0, nc, step, 0)

    def drain_form(form):
        def step(u, carry):
            for e in range(2):
                sent(2 * u + e == r, *gather_copy(form, 2 * u + e, e))
                sent((2 * c + e == r) & (u == c), *near_copy(form, u, e))
            return carry
        lax.fori_loop(0, nc, step, 0)

    send_form(0)
    bias_swap.start()
    send_form(1)

    for form, w in enumerate((ws, we)):
        wvt[form] = w[:, 2 * channels : 3 * channels].astype(F32).T.astype(BF16)
        wgt[form] = w[:, 3 * channels : 4 * channels].astype(F32).T.astype(BF16)

    def mask_row(t):
        return tm[pl.ds(t, 1), :].astype(F32)

    def penalty(t):
        return (mask_row(t) - 1.0) * 1e9

    for g in range(2):
        row_bias = penalty(2 * c + g)
        for h in range(heads):
            part = (bs[h, :, g * tile : (g + 1) * tile].astype(F32) + row_bias) * LOG2E
            bias[0, h, g * tile : (g + 1) * tile, :] = part.T

    bias_swap.wait_recv()
    for part_ref, rows, t in (
        (be.at[:, :, mine], mine, r),
        (be_in, other, mate),
    ):
        column = jnp.broadcast_to(penalty(t), (tile, tile)).T
        for h in range(heads):
            bias[1, h, rows, :] = (part_ref[h].astype(F32) + column) * LOG2E

    scale = depth ** (-0.5) * LOG2E
    lane = lax.broadcasted_iota(jnp.int32, (tile, channels), 1) // depth
    ones = jnp.ones((16, 2 * tile), BF16)

    def attend(form, w, a):
        rows = kv[form, a]
        keys = nn(rows, w[:, channels : 2 * channels]).astype(BF16)
        values = nt(wvt[form], rows).astype(BF16)
        query = nn(q[form, a], w[:, :channels]) * scale
        for h in range(heads):
            chosen = jnp.where(lane == h, query, 0.0).astype(BF16)
            scores = nt(keys, chosen) + bias[form, h]
            peak = jnp.max(scores, axis=0, keepdims=True)
            probs = jnp.exp2(scores - peak).astype(BF16)
            lhs = jnp.concatenate([values[h * depth : (h + 1) * depth], ones], axis=0)
            total = nn(lhs, probs)
            pn[form, a, h * depth : (h + 1) * depth, :] = total[:depth].astype(BF16)
            pst[form, a, h : h + 1, :] = peak
            pst[form, a, heads + h : heads + h + 1, :] = total[depth : depth + 1]

    def landed(dst, recv):
        remote(dst, dst, sf.at[0, 0], recv, mate, c).wait_recv()

    own_sem = (rg, rn)
    far_sem = (rn, rg)

    def forward(form, a):
        piece = kv.at[form, a, mine]
        landed(piece, own_sem[form].at[form, a])
        remote(piece, piece, sf.at[form, a], rf.at[form, a], mate, c).start()

    def partial_copies(form, a):
        src_n, src_s = pn.at[form, a], pst.at[form, a]
        sems = (spn.at[form, a], sps.at[form, a])
        if form == 0:
            to, b = a // per, lax.rem(a, per)
            return (
                to == c, r, to,
                (src_n, rsn.at[c, b], sems[0], rsn_sem.at[c, b]),
                (src_s, rss.at[c, b], sems[1], rss_sem.at[c, b]),
            )
        return (
            a == r, a, c,
            (src_n, ren.at[r], sems[0], ren_sem.at[r]),
            (src_s, res.at[r], sems[1], res_sem.at[r]),
        )

    def run_form(form, w):
        look = LOOK if form == 0 else n

        def ahead(t, carry):
            forward(form, turn(t))
            return carry

        lax.fori_loop(0, look, ahead, 0)

        def step(t, carry):
            a = turn(t)
            if look < n:
                @pl.when(t + look < n)
                def _():
                    forward(form, turn(t + look))
            landed(q.at[form, a], far_sem[form].at[form, a])
            landed(kv.at[form, a, other], rf.at[form, a])
            attend(form, w, a)
            here, row, col, numer, stats = partial_copies(form, a)
            either(here, *numer, row, col)
            either(here, *stats, row, col)
            return carry

        lax.fori_loop(0, n, step, 0)

    def combine(parts, stats):
        peaks = [s[:heads] for s in stats]
        largest = functools.reduce(jnp.maximum, peaks)
        factors = [jnp.exp2(p - largest) for p in peaks]
        denom = sum(f * s[heads:] for f, s in zip(factors, stats))
        rows = []
        for h in range(heads):
            pick = slice(h * depth, (h + 1) * depth)
            total = sum(f[h : h + 1] * p[pick].astype(F32) for f, p in zip(factors, parts))
            rows.append(total / denom[h : h + 1])
        return jnp.concatenate(rows, axis=0)

    def finish(form, attended, rows, weight, mask):
        gate = nt(wgt[form], rows)
        gated = jax.nn.sigmoid(gate) * attended * mask
        return nn(gated.T.astype(BF16), weight).astype(BF16)

    run_form(0, ws)
    run_form(1, we)

    for b in range(per):
        a = per * c + b
        for g in range(nc):
            landed(rsn.at[g, b], rsn_sem.at[g, b])
            landed(rss.at[g, b], rss_sem.at[g, b])
        attended = combine([rsn[g, b] for g in range(nc)], [rss[g, b] for g in range(nc)])
        mask = mask_row(r) * tms[offs[0] + a].astype(F32)
        out_s[b] = finish(0, attended, q[0, a], wso[...], mask)

    for e in range(2):
        for m in range(nc):
            landed(ren.at[2 * m + e], ren_sem.at[2 * m + e])
            landed(res.at[2 * m + e], res_sem.at[2 * m + e])
        attended = combine(
            [ren[2 * m + e] for m in range(nc)], [res[2 * m + e] for m in range(nc)]
        )
        mask = mask_row(2 * c + e) * tms[offs[1] + r].astype(F32)
        rows = x[1, e * tile : (e + 1) * tile, :]
        out_e[0, e * tile : (e + 1) * tile, :] = finish(1, attended, rows, weo[...], mask)

    bias_swap.wait_send()
    for form in range(2):
        drain_form(form)

        def drain(a, carry):
            piece = kv.at[form, a, mine]
            remote(piece, piece, sf.at[form, a], rf.at[form, a], mate, c).wait_send()
            here, _, _, numer, stats = partial_copies(form, a)
            sent(here, *numer)
            sent(here, *stats)
            return carry

        lax.fori_loop(0, n, drain, 0)


def local(z_rows, z_cols, bias_start, bias_end, w_start_in, w_start_out, w_end_in, w_end_out, token_mask, offsets):
    n, nc = lax.axis_size("row"), lax.axis_size("col")
    heads, tile, span = bias_start.shape
    channels = z_rows.shape[2]
    per = n // nc
    vmem = pl.BlockSpec(memory_space=pltpu.VMEM)
    smem = pl.BlockSpec(memory_space=pltpu.SMEM)
    dma = pltpu.SemaphoreType.DMA
    return pl.pallas_call(
        functools.partial(kernel, n, nc, heads),
        out_shape=(
            jax.ShapeDtypeStruct((per, tile, channels), BF16),
            jax.ShapeDtypeStruct((1, span, channels), BF16),
        ),
        in_specs=[vmem] * 9 + [smem] * 2,
        out_specs=(vmem, vmem),
        scratch_shapes=[
            pltpu.VMEM((2, span, channels), BF16),
            pltpu.VMEM((2, n, span, channels), BF16),
            pltpu.VMEM((2, n, tile, channels), BF16),
            pltpu.VMEM((2, heads, span, tile), F32),
            pltpu.VMEM((2, channels, channels), BF16),
            pltpu.VMEM((2, channels, channels), BF16),
            pltpu.VMEM((heads, tile, tile), BF16),
            pltpu.VMEM((2, n, channels, tile), BF16),
            pltpu.VMEM((2, n, 2 * heads, tile), F32),
            pltpu.VMEM((nc, per, channels, tile), BF16),
            pltpu.VMEM((nc, per, 2 * heads, tile), F32),
            pltpu.VMEM((n, channels, tile), BF16),
            pltpu.VMEM((n, 2 * heads, tile), F32),
            dma((2, n)), dma((2, n)), dma((2, n)), dma((2, n)), dma((2, n)), dma,
            dma((2, n)), dma((2, n)), dma((2, n)),
            dma((nc, per)), dma((nc, per)), dma((n,)), dma((n,)), dma,
        ],
        compiler_params=pltpu.CompilerParams(
            collective_id=0, has_side_effects=True, vmem_limit_bytes=32 * 1024 * 1024
        ),
        name="triangle_attention",
    )(
        z_rows, z_cols, bias_start, bias_end, w_start_in, w_start_out, w_end_in, w_end_out,
        token_mask.reshape(-1, tile), token_mask, offsets,
    )


def solution(mesh):
    return jax.shard_map(
        local,
        mesh=mesh,
        in_specs=(
            P("row", "col", None),
            P("row", "col", None),
            P(None, "row", "col"),
            P(None, "row", "col"),
            P(),
            P(),
            P(),
            P(),
            P(),
            P(),
        ),
        out_specs=(P("col", "row", None), P("row", "col", None)),
        check_vma=False,
    )
```

time: 693 us -> 111 us (0.16)
  waiting for transfers between devices: 248 us -> 0 us
  local copies, waits for them, and re-layouts: 179 us -> 9.5 us
  blocking collectives: 101 us -> 0 us
  Pallas kernels: 0 us -> 100 us
  other arithmetic: 90.5 us -> 0 us
  matrix products: 29.3 us -> 0 us
  starting transfers between devices: 23.8 us -> 0 us
  between operations: 16 us -> 0.66 us
    all_gather x7 -> x0, waiting for transfers between devices: 229 us -> none  [the longest x4 229 us: joined(): everything = jax.tree.map(lambda part: lax.all_gather(part, axis), value)]
    dynamic_slice x94 -> x0, local copies, waits for them, and re-layouts: 117 us -> none  [the longest x66 107 us: step(): return combine(so_far, jax.tree.map(lambda part: part[k], everything))]
    all_gather x4 -> x0, blocking collectives: 101 us -> none  [the longest x2 51 us: joined(): everything = jax.tree.map(lambda part: lax.all_gather(part, axis), value)]
    pallas_call x0 -> x1, Pallas kernels: none -> 100 us  [local(): pl.pallas_call(functools.partial(kernel, n, nc, heads), out_shape=(jax.Sh...]
    add x44 -> x0, other arithmetic: 54.2 us -> none  [the longest x22 51.7 us: combine_parts(): spread_heads(earlier[1], early_factor)]
    dot_general x40 -> x0, matrix products: 29.3 us -> none  [the longest x8 9.03 us: end_block(): jnp.einsum('ahkb,akhd->abhd', exponent.astype(jnp.bfloat16), value_rows,...]
    all_to_all x2 -> x0, starting transfers between devices: 23.1 us -> none  [the longest x1 12.6 us: local(): lax.all_to_all(wide_end, 'row', split_axis=1, concat_axis=0, tiled=True)]
    unnamed x2 -> x0, other arithmetic: 22.9 us -> none
  transfers between devices with their start and end apart: 9 -> 0, of which waited for: 4 -> 0; matrix products, arithmetic and copies ran while one was open for 21% -> 0% of each run, Pallas kernels for 0% -> 0%
where the time goes in v1:
time: 111 us; the launch traced here: 110 us
  Pallas kernels  100 us (90%)
  local copies, waits for them, and re-layouts  9.5 us (9%)
    pallas_call x1, Pallas kernels, local(): pl.pallas_call(functools.partial(kernel, n, nc, heads), out_shape=(jax.Sh...  100 us
    unnamed x22, local copies, waits for them, and re-layouts  9.5 us

profile of v1, /device:TPU:1, one launch (start us, length us, event | category | flops | bytes accessed | tf_op | source)
XLA Modules:
  0.0 110.2 jit_solution(16735357871424992817)
XLA Ops:
  0.6 0.0 copy-start.9
  0.6 0.6 copy-done.9
  1.3 0.0 copy-start
  1.3 0.9 copy-done
  2.2 0.0 copy-start.1
  2.2 0.9 copy-done.1
  3.2 0.0 copy-start.2
  3.2 0.9 copy-done.2
  4.1 0.0 copy-start.3
  4.1 0.9 copy-done.3
  5.0 0.0 copy-start.4
  5.0 0.8 copy-done.4
  5.8 0.0 copy-start.5
  5.8 0.8 copy-done.5
  6.7 0.0 copy-start.6
  6.7 0.7 copy-done.6
  7.4 0.0 copy-start.7
  7.4 0.8 copy-done.7
  8.1 0.0 copy-start.8
  8.1 0.8 copy-done.8
  8.9 100.1 %triangle_attention.1 = (bf16[2,128,128]{2,1,0:T(8,128)(2,1)S(1)}, bf16[1,256,128]{2,1,0:T(8,128)(2,1)S(1)}) custom-call(bf16[1,256,128]{2,1,0:T(8,128)(2,1)S(1)} %copy-done.4, bf16[1,256,128]{2,1,0:T(8,128)(2,1)S(1)} %copy-done.5, bf16[4,128,256]{2,1,0:T(8,128)(2,1)S(1)} %copy-done, bf16[4,128,256]{2,1,0:T(8,128)(2,1)S(1)} %copy-done.1, ...), custom_call_target="tpu_custom_call" | custom-call | tf_op jit(solution)/shard_map/triangle_attention/pallas_call | solution.py:315
  109.0 0.6 copy.14
  109.6 0.6 copy.15
Async XLA Ops:
  0.6 0.7 copy-start.9
  1.3 0.9 copy-start
  2.2 0.9 copy-start.1
  3.2 0.9 copy-start.2
  4.1 0.9 copy-start.3
  5.0 0.8 copy-start.4
  5.8 0.8 copy-start.5
  6.7 0.7 copy-start.6
  7.4 0.8 copy-start.7
  8.1 0.8 copy-start.8

commit v2 on v1

--- a/solution.py
+++ b/solution.py
@@ -34,9 +34,9 @@
     n, nc, heads,
     zr, zc, bs, be, ws, wso, we, weo, tm, tms, offs,
     out_s, out_e,
-    x, kv, q, bias, wvt, wgt, be_in, pn, pst, rsn, rss, ren, res,
-    sg, sn, sf, spn, sps, sb,
-    rg, rn, rf, rsn_sem, rss_sem, ren_sem, res_sem, rb,
+    cols, kv, q, bias, wvt, wgt, be_in, pn, pst, rsn, rss, ren, res,
+    sg, sn, sc, sz, sf, spn, sps, sb,
+    rg, rn, rc, rf, rsn_sem, rss_sem, ren_sem, res_sem, rb,
 ):
     r = lax.axis_index("row")
     c = lax.axis_index("col")
@@ -49,13 +49,15 @@
     per = n // nc
     mine = pl.ds(pl.multiple_of(core * tile, tile), tile)
     other = pl.ds(pl.multiple_of((1 - core) * tile, tile), tile)
-    diagonal = chip == c
-
-    def peer(u):
-        return lax.rem((r + 1) // 2 + u + nc - c, nc)
+    deep = nc // 2
+    lap, lane_z = c // deep, lax.rem(c, deep)
+    twin = (1 - lap) * deep + lane_z
+
+    def level(d):
+        return lap * deep + lax.rem(lane_z + d, deep)
 
     def turn(t):
-        return lax.rem(2 * (chip + c) + 2 * n - t, n)
+        return 2 * lax.rem(chip + nc - t // 2, nc) + lax.rem(t, 2)
 
     barrier = pltpu.get_barrier_semaphore()
 
@@ -73,39 +75,27 @@
     lax.fori_loop(1, n, greet_row, 0)
     lax.fori_loop(1, nc, greet_col, 0)
 
-    def greet_near(d, carry):
-        row_to, col_to = 2 * c + lax.rem(d, 2), d // 2
-        @pl.when(jnp.logical_not((row_to == r) & (col_to == c)))
-        def _():
-            greet(row_to, col_to)
-        @pl.when(jnp.logical_not((d == r) & diagonal))
-        def _():
-            greet(d, chip)
-        return carry
-
-    lax.fori_loop(0, n, greet_near, 0)
-
-    x[0] = normalize(zr[0])
-    x[1] = normalize(zc[0])
-
-    pl.semaphore_wait(barrier, n - 1 + nc - 1 + 2 * n - jnp.where(diagonal, 2, 0))
-
-    def half(form, e):
-        return x.at[form, pl.ds(e * tile, tile)]
-
-    def gather_copy(form, row_to, e):
+    cols[0, c] = normalize(zr[0])
+    cols[1, c] = normalize(zc[0])
+
+    pl.semaphore_wait(barrier, n - 1 + nc - 1)
+
+    def half(form, block, e):
+        return cols.at[form, block, pl.ds(e * tile, tile)]
+
+    def gather_copy(form, to, e):
         if form == 0:
             dst = kv.at[0, r, pl.ds(e * tile, tile)]
         else:
             dst = q.at[1, r]
-        return half(form, e), dst, sg.at[form, row_to], rg.at[form, r]
-
-    def near_copy(form, col_to, e):
+        return half(form, c, e), dst, sg.at[form, 2 * to + e], rg.at[form, r]
+
+    def near_copy(form, to, e):
         if form == 0:
             dst = q.at[0, r]
         else:
             dst = kv.at[1, r, pl.ds(e * tile, tile)]
-        return half(form, e), dst, sn.at[form, 2 * col_to + e], rn.at[form, r]
+        return half(form, to, e), dst, sn.at[form, 2 * to + e], rn.at[form, r]
 
     def remote(src, dst, send, recv, row, col):
         return pltpu.make_async_remote_copy(
@@ -130,31 +120,69 @@
         be.at[:, :, pl.ds(pl.multiple_of((1 - core) * tile, tile), tile)], be_in, sb, rb, mate, c
     )
 
-    def send_form(form):
+    def along(u):
+        return lax.rem(chip + u, nc)
+
+    def column_copies(form):
+        mine_out = [(twin, sc.at[form, 0])] + [(level(d), sc.at[form, d]) for d in range(1, deep)]
+        own = cols.at[form, c]
+        return [remote(own, own, sem, rc.at[form, c], r, to) for to, sem in mine_out]
+
+    def relay_copies(form):
+        other_block = cols.at[form, twin]
+        return [
+            remote(other_block, other_block, sz.at[form, d], rc.at[form, twin], r, level(d))
+            for d in range(1, deep)
+        ]
+
+    def relay(form):
+        landed(cols.at[form, twin], rc.at[form, twin])
+        for copy in relay_copies(form):
+            copy.start()
+
+    def send_gather(form):
         def step(u, carry):
-            to = peer(u)
+            to = along(u)
             for e in range(2):
-                either(2 * to + e == r, *gather_copy(form, 2 * to + e, e), 2 * to + e, c)
-                here = (2 * c + e == r) & (to == c)
-                either(here, *near_copy(form, to, e), 2 * c + e, to)
+                either((u == 0) & (core == e), *gather_copy(form, to, e), 2 * to + e, c)
             return carry
         lax.fori_loop(0, nc, step, 0)
 
+    def send_near(form, u):
+        to = along(u)
+        @pl.when((to != c) & (to != twin))
+        def _():
+            landed(cols.at[form, to], rc.at[form, to])
+        for e in range(2):
+            either((u == 0) & (core == e), *near_copy(form, to, e), 2 * to + e, c)
+
     def drain_form(form):
+        for copy in column_copies(form) + relay_copies(form):
+            copy.wait_send()
         def step(u, carry):
+            to = along(u)
             for e in range(2):
-                sent(2 * u + e == r, *gather_copy(form, 2 * u + e, e))
-                sent((2 * c + e == r) & (u == c), *near_copy(form, u, e))
+                here = (u == 0) & (core == e)
+                sent(here, *gather_copy(form, to, e))
+                sent(here, *near_copy(form, to, e))
             return carry
         lax.fori_loop(0, nc, step, 0)
 
-    send_form(0)
+    def landed(dst, recv):
+        remote(dst, dst, sf.at[0, 0], recv, mate, c).wait_recv()
+
+    for copy in column_copies(0):
+        copy.start()
     bias_swap.start()
-    send_form(1)
+    send_gather(0)
 
     for form, w in enumerate((ws, we)):
         wvt[form] = w[:, 2 * channels : 3 * channels].astype(F32).T.astype(BF16)
         wgt[form] = w[:, 3 * channels : 4 * channels].astype(F32).T.astype(BF16)
+
+    relay(0)
+    for copy in column_copies(1):
+        copy.start()
 
     def mask_row(t):
         return tm[pl.ds(t, 1), :].astype(F32)
@@ -167,6 +195,14 @@
         for h in range(heads):
             part = (bs[h, :, g * tile : (g + 1) * tile].astype(F32) + row_bias) * LOG2E
             bias[0, h, g * tile : (g + 1) * tile, :] = part.T
+
+    def near_0(u, carry):
+        send_near(0, u)
+        return carry
+
+    lax.fori_loop(0, nc, near_0, 0)
+    relay(1)
+    send_gather(1)
 
     bias_swap.wait_recv()
     for part_ref, rows, t in (
@@ -197,9 +233,6 @@
             pst[form, a, h : h + 1, :] = peak
             pst[form, a, heads + h : heads + h + 1, :] = total[depth : depth + 1]
 
-    def landed(dst, recv):
-        remote(dst, dst, sf.at[0, 0], recv, mate, c).wait_recv()
-
     own_sem = (rg, rn)
     far_sem = (rn, rg)
 
@@ -235,6 +268,10 @@
 
         def step(t, carry):
             a = turn(t)
+            if form == 0:
+                @pl.when(t < nc)
+                def _():
+                    send_near(1, t)
             if look < n:
                 @pl.when(t + look < n)
                 def _():
@@ -286,7 +323,7 @@
             [ren[2 * m + e] for m in range(nc)], [res[2 * m + e] for m in range(nc)]
         )
         mask = mask_row(2 * c + e) * tms[offs[1] + r].astype(F32)
-        rows = x[1, e * tile : (e + 1) * tile, :]
+        rows = cols[1, c, e * tile : (e + 1) * tile, :]
         out_e[0, e * tile : (e + 1) * tile, :] = finish(1, attended, rows, weo[...], mask)
 
     bias_swap.wait_send()
@@ -321,7 +358,7 @@
         in_specs=[vmem] * 9 + [smem] * 2,
         out_specs=(vmem, vmem),
         scratch_shapes=[
-            pltpu.VMEM((2, span, channels), BF16),
+            pltpu.VMEM((2, nc, span, channels), BF16),
             pltpu.VMEM((2, n, span, channels), BF16),
             pltpu.VMEM((2, n, tile, channels), BF16),
             pltpu.VMEM((2, heads, span, tile), F32),
@@ -334,8 +371,8 @@
             pltpu.VMEM((nc, per, 2 * heads, tile), F32),
             pltpu.VMEM((n, channels, tile), BF16),
             pltpu.VMEM((n, 2 * heads, tile), F32),
-            dma((2, n)), dma((2, n)), dma((2, n)), dma((2, n)), dma((2, n)), dma,
-            dma((2, n)), dma((2, n)), dma((2, n)),
+            dma((2, n)), dma((2, n)), dma((2, nc)), dma((2, nc)), dma((2, n)), dma((2, n)), dma((2, n)), dma,
+            dma((2, n)), dma((2, n)), dma((2, nc)), dma((2, n)),
             dma((nc, per)), dma((nc, per)), dma((n,)), dma((n,)), dma,
         ],
         compiler_params=pltpu.CompilerParams(

time: 111 us -> 84.2 us (0.76)
  Pallas kernels: 100 us -> 73.6 us
    pallas_call x1, Pallas kernels: 100 us -> 73.6 us  [local(): pl.pallas_call(functools.partial(kernel, n, nc, heads), out_shape=(jax.Sh...]
where the time goes in v2:
time: 84.2 us; the launch traced here: 83.7 us
  Pallas kernels  73.6 us (87%)
  local copies, waits for them, and re-layouts  9.5 us (11%)
    pallas_call x1, Pallas kernels, local(): pl.pallas_call(functools.partial(kernel, n, nc, heads), out_shape=(jax.Sh...  73.6 us
    unnamed x22, local copies, waits for them, and re-layouts  9.5 us

profile of v2, /device:TPU:1, one launch (start us, length us, event | category | flops | bytes accessed | tf_op | source)
XLA Modules:
  0.0 83.7 jit_solution(144357892818966558)
XLA Ops:
  0.6 0.0 copy-start.9
  0.6 0.6 copy-done.9
  1.3 0.0 copy-start
  1.3 0.9 %copy-done = bf16[4,128,256]{2,1,0:T(8,128)(2,1)S(1)} copy-done((bf16[4,128,256]{2,1,0:T(8,128)(2,1)S(1)}, bf16[4,128,256]{2,1,0:T(8,128)(2,1)}, u32[]{:S(2)}) %copy-start) | copy-done | bytes 262168
  2.2 0.0 copy-start.1
  2.2 0.9 %copy-done.1 = bf16[4,128,256]{2,1,0:T(8,128)(2,1)S(1)} copy-done((bf16[4,128,256]{2,1,0:T(8,128)(2,1)S(1)}, bf16[4,128,256]{2,1,0:T(8,128)(2,1)}, u32[]{:S(2)}) %copy-start.1) | copy-done | bytes 262168
  3.2 0.0 copy-start.2
  3.2 0.9 %copy-done.2 = bf16[128,512]{1,0:T(8,128)(2,1)S(1)} copy-done((bf16[128,512]{1,0:T(8,128)(2,1)S(1)}, bf16[128,512]{1,0:T(8,128)(2,1)}, u32[]{:S(2)}) %copy-start.2) | copy-done | bytes 131096
  4.1 0.0 copy-start.3
  4.1 0.9 %copy-done.3 = bf16[128,512]{1,0:T(8,128)(2,1)S(1)} copy-done((bf16[128,512]{1,0:T(8,128)(2,1)S(1)}, bf16[128,512]{1,0:T(8,128)(2,1)}, u32[]{:S(2)}) %copy-start.3) | copy-done | bytes 131096
  5.0 0.0 copy-start.4
  5.0 0.8 copy-done.4
  5.8 0.0 copy-start.5
  5.8 0.8 copy-done.5
  6.7 0.0 copy-start.6
  6.7 0.7 copy-done.6
  7.4 0.0 copy-start.7
  7.4 0.8 copy-done.7
  8.1 0.0 copy-start.8
  8.1 0.8 copy-done.8
  8.9 73.6 %triangle_attention.1 = (bf16[2,128,128]{2,1,0:T(8,128)(2,1)S(1)}, bf16[1,256,128]{2,1,0:T(8,128)(2,1)S(1)}) custom-call(bf16[1,256,128]{2,1,0:T(8,128)(2,1)S(1)} %copy-done.4, bf16[1,256,128]{2,1,0:T(8,128)(2,1)S(1)} %copy-done.5, bf16[4,128,256]{2,1,0:T(8,128)(2,1)S(1)} %copy-done, bf16[4,128,256]{2,1,0:T(8,128)(2,1)S(1)} %copy-done.1, ...), custom_call_target="tpu_custom_call" | custom-call | tf_op jit(solution)/shard_map/triangle_attention/pallas_call | solution.py:352
  82.5 0.6 copy.14
  83.1 0.6 copy.15
Async XLA Ops:
  0.6 0.7 copy-start.9
  1.3 0.9 %copy-start = (bf16[4,128,256]{2,1,0:T(8,128)(2,1)S(1)}, bf16[4,128,256]{2,1,0:T(8,128)(2,1)}, u32[]{:S(2)}) copy-start(bf16[4,128,256]{2,1,0:T(8,128)(2,1)} %bs.1) | copy-start | bytes 786436
  2.2 0.9 %copy-start.1 = (bf16[4,128,256]{2,1,0:T(8,128)(2,1)S(1)}, bf16[4,128,256]{2,1,0:T(8,128)(2,1)}, u32[]{:S(2)}) copy-start(bf16[4,128,256]{2,1,0:T(8,128)(2,1)} %be.1) | copy-start | bytes 786436
  3.2 0.9 %copy-start.2 = (bf16[128,512]{1,0:T(8,128)(2,1)S(1)}, bf16[128,512]{1,0:T(8,128)(2,1)}, u32[]{:S(2)}) copy-start(bf16[128,512]{1,0:T(8,128)(2,1)} %ws.1) | copy-start | bytes 393220
  4.1 0.9 %copy-start.3 = (bf16[128,512]{1,0:T(8,128)(2,1)S(1)}, bf16[128,512]{1,0:T(8,128)(2,1)}, u32[]{:S(2)}) copy-start(bf16[128,512]{1,0:T(8,128)(2,1)} %we.1) | copy-start | bytes 393220
  5.0 0.8 %copy-start.4 = (bf16[1,256,128]{2,1,0:T(8,128)(2,1)S(1)}, bf16[1,256,128]{2,1,0:T(8,128)(2,1)}, u32[]{:S(2)}) copy-start(bf16[1,256,128]{2,1,0:T(8,128)(2,1)} %zr.1) | copy-start | bytes 196612
  5.8 0.8 %copy-start.5 = (bf16[1,256,128]{2,1,0:T(8,128)(2,1)S(1)}, bf16[1,256,128]{2,1,0:T(8,128)(2,1)}, u32[]{:S(2)}) copy-start(bf16[1,256,128]{2,1,0:T(8,128)(2,1)} %zc.1) | copy-start | bytes 196612
  6.7 0.7 copy-start.6
  7.4 0.8 copy-start.7
  8.1 0.8 copy-start.8

commit v3 on v2

--- a/solution.py
+++ b/solution.py
@@ -10,7 +10,7 @@
 
 MESH = pl.DeviceIdType.MESH
 LOG2E = math.log2(math.e)
-LOOK = 2
+BATCH = 4
 F32 = jnp.float32
 BF16 = jnp.bfloat16
 
@@ -32,9 +32,10 @@
 
 def kernel(
     n, nc, heads,
-    zr, zc, bs, be, ws, wso, we, weo, tm, tms, offs,
+    zr_in, zc_in, bs_in, be_far, ws_in, wso_in, we_in, weo_in, tm_in, tms, offs,
     out_s, out_e,
-    cols, kv, q, bias, wvt, wgt, be_in, pn, pst, rsn, rss, ren, res,
+    zr, zc, bs, be, ws, wso, we, weo, tm, got,
+    cols, kv, q, bias, wgt, be_in, pn, pst, rsn, rss, ren, res,
     sg, sn, sc, sz, sf, spn, sps, sb,
     rg, rn, rc, rf, rsn_sem, rss_sem, ren_sem, res_sem, rb,
 ):
@@ -45,6 +46,7 @@
     mate = r + 1 - 2 * core
     tile = tm.shape[1]
     channels = zr.shape[2]
+    batch = min(BATCH, n)
     depth = channels // heads
     per = n // nc
     mine = pl.ds(pl.multiple_of(core * tile, tile), tile)
@@ -59,6 +61,16 @@
     def turn(t):
         return 2 * lax.rem(chip + nc - t // 2, nc) + lax.rem(t, 2)
 
+    fetches = [
+        pltpu.make_async_copy(src, dst, got.at[k])
+        for k, (src, dst) in enumerate((
+            (zr_in, zr), (zc_in, zc), (ws_in, ws), (we_in, we), (tm_in, tm), (bs_in, bs),
+            (be_far.at[:, :, mine], be), (wso_in, wso), (weo_in, weo),
+        ))
+    ]
+    for fetch in fetches:
+        fetch.start()
+
     barrier = pltpu.get_barrier_semaphore()
 
     def greet(row, col):
@@ -75,7 +87,9 @@
     lax.fori_loop(1, n, greet_row, 0)
     lax.fori_loop(1, nc, greet_col, 0)
 
+    fetches[0].wait()
     cols[0, c] = normalize(zr[0])
+    fetches[1].wait()
     cols[1, c] = normalize(zc[0])
 
     pl.semaphore_wait(barrier, n - 1 + nc - 1)
@@ -117,7 +131,7 @@
             remote(src, dst, send, recv, mate, c).wait_send()
 
     bias_swap = remote(
-        be.at[:, :, pl.ds(pl.multiple_of((1 - core) * tile, tile), tile)], be_in, sb, rb, mate, c
+        be_far.at[:, :, other], be_in, sb, rb, mate, c
     )
 
     def along(u):
@@ -176,8 +190,9 @@
     bias_swap.start()
     send_gather(0)
 
+    for fetch in fetches[2:]:
+        fetch.wait()
     for form, w in enumerate((ws, we)):
-        wvt[form] = w[:, 2 * channels : 3 * channels].astype(F32).T.astype(BF16)
         wgt[form] = w[:, 3 * channels : 4 * channels].astype(F32).T.astype(BF16)
 
     relay(0)
@@ -190,11 +205,9 @@
     def penalty(t):
         return (mask_row(t) - 1.0) * 1e9
 
-    for g in range(2):
-        row_bias = penalty(2 * c + g)
-        for h in range(heads):
-            part = (bs[h, :, g * tile : (g + 1) * tile].astype(F32) + row_bias) * LOG2E
-            bias[0, h, g * tile : (g + 1) * tile, :] = part.T
+    key_bias = jnp.concatenate([penalty(2 * c), penalty(2 * c + 1)], axis=1)
+    for h in range(heads):
+        bias[0, h] = (bs[h].astype(F32) + key_bias) * LOG2E
 
     def near_0(u, carry):
         send_near(0, u)
@@ -205,33 +218,42 @@
     send_gather(1)
 
     bias_swap.wait_recv()
-    for part_ref, rows, t in (
-        (be.at[:, :, mine], mine, r),
-        (be_in, other, mate),
-    ):
-        column = jnp.broadcast_to(penalty(t), (tile, tile)).T
+    for part, cols_at, t in ((be, mine, r), (be_in, other, mate)):
+        row = penalty(t)
         for h in range(heads):
-            bias[1, h, rows, :] = (part_ref[h].astype(F32) + column) * LOG2E
+            bias[1, h, :, cols_at] = (part[h].astype(F32).T + row) * LOG2E
 
     scale = depth ** (-0.5) * LOG2E
-    lane = lax.broadcasted_iota(jnp.int32, (tile, channels), 1) // depth
-    ones = jnp.ones((16, 2 * tile), BF16)
-
-    def attend(form, w, a):
-        rows = kv[form, a]
-        keys = nn(rows, w[:, channels : 2 * channels]).astype(BF16)
-        values = nt(wvt[form], rows).astype(BF16)
-        query = nn(q[form, a], w[:, :channels]) * scale
-        for h in range(heads):
-            chosen = jnp.where(lane == h, query, 0.0).astype(BF16)
-            scores = nt(keys, chosen) + bias[form, h]
-            peak = jnp.max(scores, axis=0, keepdims=True)
-            probs = jnp.exp2(scores - peak).astype(BF16)
-            lhs = jnp.concatenate([values[h * depth : (h + 1) * depth], ones], axis=0)
-            total = nn(lhs, probs)
-            pn[form, a, h * depth : (h + 1) * depth, :] = total[:depth].astype(BF16)
-            pst[form, a, h : h + 1, :] = peak
-            pst[form, a, heads + h : heads + h + 1, :] = total[depth : depth + 1]
+    lane = lax.broadcasted_iota(jnp.int32, (tile, channels), 1)
+    head_of = lane // depth
+    ones = jnp.ones((2 * tile, channels), BF16)
+
+    def attend(form, w, turns):
+        rows = jnp.concatenate([kv[form, a] for a in turns], axis=0)
+        both = nn(rows, w[:, channels : 3 * channels]).astype(BF16)
+        rows = jnp.concatenate([q[form, a] for a in turns], axis=0)
+        queries = nn(rows, w[:, :channels]) * scale
+        for i, a in enumerate(turns):
+            keys = both[2 * i * tile : 2 * (i + 1) * tile, :channels]
+            values = both[2 * i * tile : 2 * (i + 1) * tile, channels:]
+            query = queries[i * tile : (i + 1) * tile]
+            chosen = [jnp.where(head_of == h, query, 0.0).astype(BF16) for h in range(heads)]
+            scores = nt(jnp.concatenate(chosen, axis=0), keys)
+            stats = jnp.zeros((tile, channels), F32)
+            probs = []
+            for h in range(heads):
+                part = scores[h * tile : (h + 1) * tile] + bias[form, h]
+                peak = jnp.max(part, axis=1, keepdims=True)
+                probs.append(jnp.exp2(part - peak).astype(BF16))
+                stats = jnp.where(lane == h, peak, stats)
+            totals = nn(jnp.concatenate(probs, axis=0), jnp.concatenate([values, ones], axis=1))
+            numer = jnp.zeros((tile, channels), F32)
+            for h in range(heads):
+                part = totals[h * tile : (h + 1) * tile]
+                numer = jnp.where(head_of == h, part[:, :channels], numer)
+                stats = jnp.where(lane == heads + h, part[:, channels:], stats)
+            pn[form, a] = numer.T.astype(BF16)
+            pst[form, a] = stats.T[: 2 * heads]
 
     own_sem = (rg, rn)
     far_sem = (rn, rg)
@@ -258,33 +280,33 @@
         )
 
     def run_form(form, w):
-        look = LOOK if form == 0 else n
-
-        def ahead(t, carry):
-            forward(form, turn(t))
+        def ahead(b):
+            for k in range(batch):
+                forward(form, turn(batch * b + k))
+
+        ahead(0)
+
+        def step(b, carry):
+            turns = [turn(batch * b + k) for k in range(batch)]
+            if form == 0:
+                @pl.when(batch * b < nc)
+                def _():
+                    for k in range(min(batch, nc)):
+                        send_near(1, batch * b + k)
+            @pl.when(batch * (b + 1) < n)
+            def _():
+                ahead(b + 1)
+            for a in turns:
+                landed(q.at[form, a], far_sem[form].at[form, a])
+                landed(kv.at[form, a, other], rf.at[form, a])
+            attend(form, w, turns)
+            for a in turns:
+                here, row, col, numer, stats = partial_copies(form, a)
+                either(here, *numer, row, col)
+                either(here, *stats, row, col)
             return carry
 
-        lax.fori_loop(0, look, ahead, 0)
-
-        def step(t, carry):
-            a = turn(t)
-            if form == 0:
-                @pl.when(t < nc)
-                def _():
-                    send_near(1, t)
-            if look < n:
-                @pl.when(t + look < n)
-                def _():
-                    forward(form, turn(t + look))
-            landed(q.at[form, a], far_sem[form].at[form, a])
-            landed(kv.at[form, a, other], rf.at[form, a])
-            attend(form, w, a)
-            here, row, col, numer, stats = partial_copies(form, a)
-            either(here, *numer, row, col)
-            either(here, *stats, row, col)
-            return carry
-
-        lax.fori_loop(0, n, step, 0)
+        lax.fori_loop(0, n // batch, step, 0)
 
     def combine(parts, stats):
         peaks = [s[:heads] for s in stats]
@@ -355,14 +377,23 @@
             jax.ShapeDtypeStruct((per, tile, channels), BF16),
             jax.ShapeDtypeStruct((1, span, channels), BF16),
         ),
-        in_specs=[vmem] * 9 + [smem] * 2,
+        in_specs=[pl.BlockSpec(memory_space=pl.ANY)] * 9 + [smem] * 2,
         out_specs=(vmem, vmem),
         scratch_shapes=[
+            pltpu.VMEM(z_rows.shape, BF16),
+            pltpu.VMEM(z_cols.shape, BF16),
+            pltpu.VMEM(bias_start.shape, BF16),
+            pltpu.VMEM((heads, tile, tile), BF16),
+            pltpu.VMEM(w_start_in.shape, BF16),
+            pltpu.VMEM(w_start_out.shape, BF16),
+            pltpu.VMEM(w_end_in.shape, BF16),
+            pltpu.VMEM(w_end_out.shape, BF16),
+            pltpu.VMEM((n, tile), jnp.int32),
+            dma((9,)),
             pltpu.VMEM((2, nc, span, channels), BF16),
             pltpu.VMEM((2, n, span, channels), BF16),
             pltpu.VMEM((2, n, tile, channels), BF16),
-            pltpu.VMEM((2, heads, span, tile), F32),
-            pltpu.VMEM((2, channels, channels), BF16),
+            pltpu.VMEM((2, heads, tile, span), F32),
             pltpu.VMEM((2, channels, channels), BF16),
             pltpu.VMEM((heads, tile, tile), BF16),
             pltpu.VMEM((2, n, channels, tile), BF16),
@@ -376,7 +407,7 @@
             dma((nc, per)), dma((nc, per)), dma((n,)), dma((n,)), dma,
         ],
         compiler_params=pltpu.CompilerParams(
-            collective_id=0, has_side_effects=True, vmem_limit_bytes=32 * 1024 * 1024
+            collective_id=0, has_side_effects=True, vmem_limit_bytes=62 * 1024 * 1024
         ),
         name="triangle_attention",
     )(

time: 84.2 us -> 60.4 us (0.72)
  Pallas kernels: 73.6 us -> 57.4 us
  local copies, waits for them, and re-layouts: 9.5 us -> 2.14 us
    pallas_call x1, Pallas kernels: 73.6 us -> 57.4 us  [local(): pl.pallas_call(functools.partial(kernel, n, nc, heads), out_shape=(jax.Sh...]
    unnamed x22 -> x4, local copies, waits for them, and re-layouts: 9.5 us -> 2.14 us
where the time goes in v3:
time: 60.4 us; the launch traced here: 60.2 us
  Pallas kernels  57.4 us (95%)
  local copies, waits for them, and re-layouts  2.14 us (4%)
  between operations  0.65 us (1%)
    pallas_call x1, Pallas kernels, local(): pl.pallas_call(functools.partial(kernel, n, nc, heads), out_shape=(jax.Sh...  57.4 us
    unnamed x4, local copies, waits for them, and re-layouts  2.14 us

profile of v3, /device:TPU:1, one launch (start us, length us, event | category | flops | bytes accessed | tf_op | source)
XLA Modules:
  0.0 60.2 jit_solution(16084790757072434296)
XLA Ops:
  0.6 57.4 %triangle_attention.1 = (bf16[2,128,128]{2,1,0:T(8,128)(2,1)}, bf16[1,256,128]{2,1,0:T(8,128)(2,1)}) custom-call(bf16[1,256,128]{2,1,0:T(8,128)(2,1)} %zr_in.1, bf16[1,256,128]{2,1,0:T(8,128)(2,1)} %zc_in.1, bf16[4,128,256]{2,1,0:T(8,128)(2,1)} %bs_in.1, bf16[4,128,256]{2,1,0:T(8,128)(2,1)} %be_far.1, bf16[128,512]{1,0:T(8,128)(2,1)} %ws_in.1, ...), custom_call_target="tpu_custom_call" | custom-call | tf_op jit(solution)/shard_map/triangle_attention/pallas_call | solution.py:374
  58.0 0.0 copy-start
  58.0 1.5 %copy.14 = bf16[2,128,128]{2,1,0:T(8,128)(2,1)} copy(bf16[2,128,128]{2,1,0:T(8,128)(2,1)} %get-tuple-element.4) | data formatting | bytes 131072
  59.5 0.0 copy-done
  59.5 0.6 %copy.15 = bf16[1,256,128]{2,1,0:T(8,128)(2,1)} copy(bf16[1,256,128]{2,1,0:T(8,128)(2,1)S(1)} %copy-done) | data formatting | bytes 131072
Async XLA Ops:
  58.0 1.5 %copy-start = (bf16[1,256,128]{2,1,0:T(8,128)(2,1)S(1)}, bf16[1,256,128]{2,1,0:T(8,128)(2,1)}, u32[]{:S(2)}) copy-start(bf16[1,256,128]{2,1,0:T(8,128)(2,1)} %get-tuple-element.5) | copy-start | bytes 196612

commit v4 on v3

v4 whole, which is shorter than its diff:
```python
import functools
import math

import jax
import jax.numpy as jnp
from jax import lax
from jax.experimental import pallas as pl
from jax.experimental.pallas import tpu as pltpu
from jax.sharding import PartitionSpec as P

MESH = pl.DeviceIdType.MESH
LOG2E = math.log2(math.e)
BATCH = 4
F32 = jnp.float32
BF16 = jnp.bfloat16


def nn(a, b):
    return lax.dot_general(a, b, (((1,), (0,)), ((), ())), preferred_element_type=F32)


def nt(a, b):
    return lax.dot_general(a, b, (((1,), (1,)), ((), ())), preferred_element_type=F32)


def normalize(block):
    values = block.astype(F32)
    center = values - jnp.mean(values, axis=-1, keepdims=True)
    spread = jnp.mean(center * center, axis=-1, keepdims=True)
    return (center * lax.rsqrt(spread + 1e-05)).astype(BF16)


def kernel(
    n, nc, heads,
    zr_in, zc_in, bs_in, be_far, ws_in, wso_in, we_in, weo_in, tm_in, offs,
    out_s, out_e,
    zr, zc, bs, be, ws, wso, we, weo, tm, tms, got,
    x, across, scat, kv, q, bias, wgt, be_in, pn, pst, rsn, rss, ren, res,
    ss, sa, sg, sc, sf, spn, sps, sb,
    rs, ra, rg, ry, rt, rn, rf, rsn_sem, rss_sem, ren_sem, res_sem, rb,
):
    r = lax.axis_index("row")
    c = lax.axis_index("col")
    core = lax.rem(r, 2)
    chip = r // 2
    mate = r + 1 - 2 * core
    tile = tm.shape[1]
    channels = zr.shape[2]
    batch = min(BATCH, n)
    depth = channels // heads
    per = n // nc
    mine = pl.ds(pl.multiple_of(core * tile, tile), tile)
    other = pl.ds(pl.multiple_of((1 - core) * tile, tile), tile)
    deep = nc // 2
    lap, lane_z = c // deep, lax.rem(c, deep)
    twin = (1 - lap) * deep + lane_z

    def level(d):
        return lap * deep + lax.rem(lane_z + d, deep)

    groups = n // batch
    piece = tile // nc
    block = chip // 2
    facing = r + 2 - 4 * lax.rem(chip, 2)

    def group(b):
        return lax.rem(block + groups - b, groups)

    def along(u):
        return 2 * lax.rem(block + u // 2, groups) + lax.rem(chip + u, 2)

    def part(p):
        return pl.ds(pl.multiple_of(p * piece, piece), piece)

    fetches = [
        pltpu.make_async_copy(src, dst, got.at[k])
        for k, (src, dst) in enumerate((
            (zr_in, zr), (zc_in, zc), (ws_in, ws), (we_in, we), (tm_in, tm), (bs_in, bs),
            (be_far.at[:, :, mine], be), (wso_in, wso), (weo_in, weo), (tm_in, tms),
        ))
    ]
    for fetch in fetches:
        fetch.start()

    barrier = pltpu.get_barrier_semaphore()

    def greet(row, col):
        pl.semaphore_signal(barrier, inc=1, device_id=(row, col), device_id_type=MESH)

    def greet_row(d, carry):
        greet(lax.rem(r + d, n), c)
        return carry

    def greet_col(d, carry):
        greet(r, lax.rem(c + d, nc))
        return carry

    lax.fori_loop(1, n, greet_row, 0)
    lax.fori_loop(1, nc, greet_col, 0)

    fetches[0].wait()
    x[0] = normalize(zr[0]).reshape(2, tile, channels)
    fetches[1].wait()
    x[1] = normalize(zc[0]).reshape(2, tile, channels)
    for form in range(2):
        for e in range(2):
            scat[c, form, e] = x[form, e, part(c), :]

    for fetch in fetches[2:]:
        fetch.wait()
    for form, w in enumerate((ws, we)):
        wgt[form] = w[:, 3 * channels : 4 * channels].astype(F32).T.astype(BF16)

    def mask_row(t):
        return tm[pl.ds(t, 1), :].astype(F32)

    def penalty(t):
        return (mask_row(t) - 1.0) * 1e9

    key_bias = jnp.concatenate([penalty(2 * c), penalty(2 * c + 1)], axis=1)
    for h in range(heads):
        bias[0, h] = (bs[h].astype(F32) + key_bias) * LOG2E

    pl.semaphore_wait(barrier, n - 1 + nc - 1)

    def remote(src, dst, send, recv, row, col):
        return pltpu.make_async_remote_copy(
            src_ref=src, dst_ref=dst, send_sem=send, recv_sem=recv,
            device_id=(row, col), device_id_type=MESH,
        )

    def either(here, src, dst, send, recv, row, col):
        @pl.when(here)
        def _():
            pltpu.make_async_copy(src, dst, recv).start()
        @pl.when(jnp.logical_not(here))
        def _():
            remote(src, dst, send, recv, row, col).start()

    bias_swap = remote(
        be_far.at[:, :, other], be_in, sb, rb, mate, c
    )

    def landed(dst, recv):
        remote(dst, dst, sb, recv, mate, c).wait_recv()

    def gone(src, send):
        remote(src, src, send, rb, mate, c).wait_send()

    def scatter(d, carry):
        to = lax.rem(c + d, nc)
        remote(x.at[:, :, part(to)], scat.at[c], ss, rs, r, to).start()
        return carry

    def cross(form):
        def step(u, carry):
            to = along(u)
            for e in range(2):
                dst = q.at[0, r, part(c)] if form == 0 else kv.at[1, r, e, part(c)]
                src = scat.at[to, form, e]
                either((u == 0) & (core == e), src, dst, sa.at[form], ra.at[form, block], 2 * to + e, c)
            return carry
        lax.fori_loop(0, nc, step, 0)

    def near_piece(form, g, p):
        rows = pl.ds(batch * g, batch)
        return q.at[0, rows, part(p)] if form == 0 else kv.at[1, rows, core, part(p)]

    def near_twin(form, b):
        g = group(b)
        landed(q.at[0, pl.ds(0, batch), part(0)], ra.at[form, g])
        own = near_piece(form, g, c)
        remote(own, own, sc.at[form], rt.at[form, g], r, twin).start()

    def near_levels(form, b, held):
        g = group(b)
        piece_ref = near_piece(form, g, held)
        for d in range(1, deep):
            remote(piece_ref, piece_ref, sc.at[form], rn.at[form, g], r, level(d)).start()

    def relay(form, b):
        landed(near_piece(form, group(b), twin), rt.at[form, group(b)])
        near_levels(form, b, twin)

    def send_facing(form):
        remote(x.at[form], across.at[form], sg.at[form], ry.at[form], facing, c).start()

    def spread(form, held, row):
        for k in range(groups):
            to = 4 * lax.rem(block + k, groups) + 2 * lax.rem(chip, 2)
            for e in range(2):
                dst = kv.at[0, row, e] if form == 0 else q.at[1, row]
                recv = rg.at[form, block]
                if k == 0:
                    either(core == e, held.at[form, e], dst, sg.at[form], recv, to + e, c)
                else:
                    remote(held.at[form, e], dst, sg.at[form], recv, to + e, c).start()

    def spread_facing(form):
        landed(x.at[form], ry.at[form])
        spread(form, across, facing)

    lax.fori_loop(1, nc, scatter, 0)
    send_facing(0)
    spread(0, x, r)
    landed(scat.at[pl.ds(0, nc - 1)], rs)
    cross(0)
    spread_facing(0)
    cross(1)
    bias_swap.start()
    send_facing(1)

    for b in range(groups):
        near_twin(0, b)
    for b in range(groups):
        near_levels(0, b, c)
        if b:
            relay(0, b - 1)
    relay(0, groups - 1)
    spread(1, x, r)
    for b in range(groups):
        near_twin(1, b)
    for b in range(groups):
        near_levels(1, b, c)

    bias_swap.wait_recv()
    for source, cols_at, t in ((be, mine, r), (be_in, other, mate)):
        row = penalty(t)
        for h in range(heads):
            bias[1, h, :, cols_at] = (source[h].astype(F32).T + row) * LOG2E

    scale = depth ** (-0.5) * LOG2E
    lane = lax.broadcasted_iota(jnp.int32, (tile, channels), 1)
    head_of = lane // depth
    ones = jnp.ones((2 * tile, channels), BF16)

    def attend(form, w, g):
        held = pl.ds(batch * g, batch)
        rows = kv[form, held].reshape(2 * batch * tile, channels)
        both = nn(rows, w[:, channels : 3 * channels]).astype(BF16)
        rows = q[form, held].reshape(batch * tile, channels)
        queries = nn(rows, w[:, :channels]) * scale
        for i in range(batch):
            a = batch * g + i
            keys = both[2 * i * tile : 2 * (i + 1) * tile, :channels]
            values = both[2 * i * tile : 2 * (i + 1) * tile, channels:]
            query = queries[i * tile : (i + 1) * tile]
            chosen = [jnp.where(head_of == h, query, 0.0).astype(BF16) for h in range(heads)]
            scores = nt(jnp.concatenate(chosen, axis=0), keys)
            stats = jnp.zeros((tile, channels), F32)
            probs = []
            for h in range(heads):
                part = scores[h * tile : (h + 1) * tile] + bias[form, h]
                peak = jnp.max(part, axis=1, keepdims=True)
                probs.append(jnp.exp2(part - peak).astype(BF16))
                stats = jnp.where(lane == h, peak, stats)
            totals = nn(jnp.concatenate(probs, axis=0), jnp.concatenate([values, ones], axis=1))
            numer = jnp.zeros((tile, channels), F32)
            for h in range(heads):
                part = totals[h * tile : (h + 1) * tile]
                numer = jnp.where(head_of == h, part[:, :channels], numer)
                stats = jnp.where(lane == heads + h, part[:, channels:], stats)
            pn[form, a] = numer.T.astype(BF16)
            pst[form, a] = stats.T[: 2 * heads]

    def forward_copy(form, g):
        held = kv.at[form, pl.ds(batch * g, batch), core]
        return remote(held, held, sf.at[form], rf.at[form, g], mate, c)

    def near_landed(form, g):
        if deep > 1:
            landed(q.at[0, pl.ds(0, (nc - 2) * batch // nc)], rn.at[form, g])

    def gather_landed(form, g):
        landed(q.at[0, pl.ds(0, batch)], rg.at[form, g])

    def forward(form, b):
        (gather_landed if form == 0 else near_landed)(form, group(b))
        forward_copy(form, group(b)).start()

    def send_partial(form, a):
        if form == 0:
            to, b = a // per, lax.rem(a, per)
            pairs = (rsn.at[c, b], rsn_sem), (rss.at[c, b], rss_sem)
            here, row, col = to == c, r, to
        else:
            pairs = (ren.at[core, chip], ren_sem.at[core]), (res.at[core, chip], res_sem.at[core])
            here, row, col = a == r, a, c
        either(here, pn.at[form, a], pairs[0][0], spn.at[form], pairs[0][1], row, col)
        either(here, pst.at[form, a], pairs[1][0], sps.at[form], pairs[1][1], row, col)

    def run_form(form, w):
        forward(form, 0)

        def step(b, carry):
            g = group(b)
            if form == 0:
                @pl.when(b == 0)
                def _():
                    spread_facing(1)
                relay(1, b)
            @pl.when(b + 1 < groups)
            def _():
                forward(form, b + 1)
            (near_landed if form == 0 else gather_landed)(form, g)
            forward_copy(form, g).wait_recv()
            if form == 1:
                for k in range(batch):
                    send_partial(0, batch * g + k)
            attend(form, w, g)
            if form == 1:
                for k in range(batch):
                    send_partial(1, batch * g + k)
            return carry

        lax.fori_loop(0, groups, step, 0)

    def combine(parts, stats):
        peaks = [s[:heads] for s in stats]
        largest = functools.reduce(jnp.maximum, peaks)
        factors = [jnp.exp2(p - largest) for p in peaks]
        denom = sum(f * s[heads:] for f, s in zip(factors, stats))
        rows = []
        for h in range(heads):
            pick = slice(h * depth, (h + 1) * depth)
            total = sum(f[h : h + 1] * p[pick].astype(F32) for f, p in zip(factors, parts))
            rows.append(total / denom[h : h + 1])
        return jnp.concatenate(rows, axis=0)

    def finish(form, attended, rows, weight, mask):
        gate = nt(wgt[form], rows)
        gated = jax.nn.sigmoid(gate) * attended * mask
        return nn(gated.T.astype(BF16), weight).astype(BF16)

    run_form(0, ws)
    run_form(1, we)

    def mask_scalar(k, a):
        at = offs[k] + a
        return tms[at // tile, lax.rem(at, tile)].astype(F32)

    landed(rsn, rsn_sem)
    landed(rss, rss_sem)
    for b in range(per):
        a = per * c + b
        attended = combine([rsn[g, b] for g in range(nc)], [rss[g, b] for g in range(nc)])
        mask = mask_row(r) * mask_scalar(0, a)
        out_s[b] = finish(0, attended, q[0, a], wso[...], mask)

    for e in range(2):
        landed(ren.at[e], ren_sem.at[e])
        landed(res.at[e], res_sem.at[e])
        attended = combine([ren[e, m] for m in range(nc)], [res[e, m] for m in range(nc)])
        mask = mask_row(2 * c + e) * mask_scalar(1, r)
        out_e[0, e * tile : (e + 1) * tile, :] = finish(1, attended, x[1, e], weo[...], mask)

    bias_swap.wait_send()
    gone(scat.at[pl.ds(0, nc - 1)], ss)
    for form in range(2):
        gone(q.at[0, pl.ds(0, n - 1), part(0)], sa.at[form])
        gone(q.at[0], sg.at[form])
        gone(q.at[0, pl.ds(0, (nc - 1) * per)], sc.at[form])
        gone(q.at[0], sf.at[form])
        remote_count = n - per if form == 0 else n - 1
        gone(pn.at[form, pl.ds(0, remote_count)], spn.at[form])
        gone(pst.at[form, pl.ds(0, remote_count)], sps.at[form])


def local(z_rows, z_cols, bias_start, bias_end, w_start_in, w_start_out, w_end_in, w_end_out, token_mask, offsets):
    n, nc = lax.axis_size("row"), lax.axis_size("col")
    heads, tile, span = bias_start.shape
    channels = z_rows.shape[2]
    per = n // nc
    groups = n // min(BATCH, n)
    vmem = pl.BlockSpec(memory_space=pltpu.VMEM)
    smem = pl.BlockSpec(memory_space=pltpu.SMEM)
    dma = pltpu.SemaphoreType.DMA
    return pl.pallas_call(
        functools.partial(kernel, n, nc, heads),
        out_shape=(
            jax.ShapeDtypeStruct((per, tile, channels), BF16),
            jax.ShapeDtypeStruct((1, span, channels), BF16),
        ),
        in_specs=[pl.BlockSpec(memory_space=pl.ANY)] * 9 + [smem],
        out_specs=(vmem, vmem),
        scratch_shapes=[
            pltpu.VMEM(z_rows.shape, BF16),
            pltpu.VMEM(z_cols.shape, BF16),
            pltpu.VMEM(bias_start.shape, BF16),
            pltpu.VMEM((heads, tile, tile), BF16),
            pltpu.VMEM(w_start_in.shape, BF16),
            pltpu.VMEM(w_start_out.shape, BF16),
            pltpu.VMEM(w_end_in.shape, BF16),
            pltpu.VMEM(w_end_out.shape, BF16),
            pltpu.VMEM((n, tile), jnp.int32),
            pltpu.SMEM((n, tile), jnp.int32),
            dma((10,)),
            pltpu.VMEM((2, 2, tile, channels), BF16),
            pltpu.VMEM((2, 2, tile, channels), BF16),
            pltpu.VMEM((nc, 2, 2, tile // nc, channels), BF16),
            pltpu.VMEM((2, n, 2, tile, channels), BF16),
            pltpu.VMEM((2, n, tile, channels), BF16),
            pltpu.VMEM((2, heads, tile, span), F32),
            pltpu.VMEM((2, channels, channels), BF16),
            pltpu.VMEM((heads, tile, tile), BF16),
            pltpu.VMEM((2, n, channels, tile), BF16),
            pltpu.VMEM((2, n, 2 * heads, tile), F32),
            pltpu.VMEM((nc, per, channels, tile), BF16),
            pltpu.VMEM((nc, per, 2 * heads, tile), F32),
            pltpu.VMEM((2, nc, channels, tile), BF16),
            pltpu.VMEM((2, nc, 2 * heads, tile), F32),
            dma, dma((2,)), dma((2,)), dma((2,)), dma((2,)), dma((2,)), dma((2,)), dma,
            dma, dma((2, groups)), dma((2, groups)), dma((2,)), dma((2, groups)), dma((2, groups)), dma((2, groups)),
            dma, dma, dma((2,)), dma((2,)), dma,
        ],
        compiler_params=pltpu.CompilerParams(
            collective_id=0, has_side_effects=True, vmem_limit_bytes=62 * 1024 * 1024
        ),
        name="triangle_attention",
    )(
        z_rows, z_cols, bias_start, bias_end, w_start_in, w_start_out, w_end_in, w_end_out,
        token_mask.reshape(-1, tile), offsets,
    )


def solution(mesh):
    return jax.shard_map(
        local,
        mesh=mesh,
        in_specs=(
            P("row", "col", None),
            P("row", "col", None),
            P(None, "row", "col"),
            P(None, "row", "col"),
            P(),
            P(),
            P(),
            P(),
            P(),
            P(),
        ),
        out_specs=(P("col", "row", None), P("row", "col", None)),
        check_vma=False,
    )
```

time: 60.4 us -> 53.3 us (0.88)
  the two profiles are of different devices: /device:TPU:1 before, /device:TPU:40 now
where the time goes in v4:
time: 53.3 us; the launch traced here: 53.2 us
  Pallas kernels  50.4 us (95%)
  local copies, waits for them, and re-layouts  2.14 us (4%)
  between operations  0.65 us (1%)
    pallas_call x1, Pallas kernels, local(): pl.pallas_call(functools.partial(kernel, n, nc, heads), out_shape=(jax.Sh...  50.4 us
    unnamed x4, local copies, waits for them, and re-layouts  2.14 us

profile of v4, /device:TPU:40, one launch (start us, length us, event | category | flops | bytes accessed | tf_op | source)
XLA Modules:
  0.0 53.2 jit_solution(3394112620685597562)
XLA Ops:
  0.6 50.4 %triangle_attention.1 = (bf16[2,128,128]{2,1,0:T(8,128)(2,1)}, bf16[1,256,128]{2,1,0:T(8,128)(2,1)}) custom-call(bf16[1,256,128]{2,1,0:T(8,128)(2,1)} %zr_in.1, bf16[1,256,128]{2,1,0:T(8,128)(2,1)} %zc_in.1, bf16[4,128,256]{2,1,0:T(8,128)(2,1)} %bs_in.1, bf16[4,128,256]{2,1,0:T(8,128)(2,1)} %be_far.1, bf16[128,512]{1,0:T(8,128)(2,1)} %ws_in.1, ...), custom_call_target="tpu_custom_call" | custom-call | tf_op jit(solution)/shard_map/triangle_attention/pallas_call | solution.py:378
  51.0 0.0 copy-start
  51.0 1.5 %copy.14 = bf16[2,128,128]{2,1,0:T(8,128)(2,1)} copy(bf16[2,128,128]{2,1,0:T(8,128)(2,1)} %get-tuple-element.4) | data formatting | bytes 131072
  52.5 0.0 copy-done
  52.5 0.6 %copy.15 = bf16[1,256,128]{2,1,0:T(8,128)(2,1)} copy(bf16[1,256,128]{2,1,0:T(8,128)(2,1)S(1)} %copy-done) | data formatting | bytes 131072
Async XLA Ops:
  51.0 1.5 %copy-start = (bf16[1,256,128]{2,1,0:T(8,128)(2,1)S(1)}, bf16[1,256,128]{2,1,0:T(8,128)(2,1)}, u32[]{:S(2)}) copy-start(bf16[1,256,128]{2,1,0:T(8,128)(2,1)} %get-tuple-element.5) | copy-start | bytes 196612

commit v5 on v4

--- a/solution.py
+++ b/solution.py
@@ -11,6 +11,7 @@
 MESH = pl.DeviceIdType.MESH
 LOG2E = math.log2(math.e)
 BATCH = 4
+MERGE = 2
 F32 = jnp.float32
 BF16 = jnp.bfloat16
 
@@ -35,9 +36,9 @@
     zr_in, zc_in, bs_in, be_far, ws_in, wso_in, we_in, weo_in, tm_in, offs,
     out_s, out_e,
     zr, zc, bs, be, ws, wso, we, weo, tm, tms, got,
-    x, across, scat, kv, q, bias, wgt, be_in, pn, pst, rsn, rss, ren, res,
+    x, across, scat, kv, q, bias, wgt, be_in, pn, pst, rsn, rss, ren, res, twn, tws, projected,
     ss, sa, sg, sc, sf, spn, sps, sb,
-    rs, ra, rg, ry, rt, rn, rf, rsn_sem, rss_sem, ren_sem, res_sem, rb,
+    rs, ra, rg, ry, rt, rn, rf, rsn_sem, rss_sem, ren_sem, res_sem, twn_sem, tws_sem, rb,
 ):
     r = lax.axis_index("row")
     c = lax.axis_index("col")
@@ -63,11 +64,25 @@
     block = chip // 2
     facing = r + 2 - 4 * lax.rem(chip, 2)
 
-    def group(b):
-        return lax.rem(block + groups - b, groups)
+    side = groups // 2
+    spans = [3, 1, 2, 0] if groups == 4 else [k % groups for k in range(1, groups + 1)]
+
+    def group(form, b):
+        if form == 0:
+            return lax.rem(block + groups - b, groups)
+        span = spans[0]
+        for k in range(1, groups):
+            span = jnp.where(b == k, spans[k], span)
+        return lax.rem(block + groups - span, groups)
 
     def along(u):
         return 2 * lax.rem(block + u // 2, groups) + lax.rem(chip + u, 2)
+
+    def mask_row(t):
+        return tm[pl.ds(t, 1), :].astype(F32)
+
+    def penalty(t):
+        return (mask_row(t) - 1.0) * 1e9
 
     def part(p):
         return pl.ds(pl.multiple_of(p * piece, piece), piece)
@@ -79,7 +94,7 @@
             (be_far.at[:, :, mine], be), (wso_in, wso), (weo_in, weo), (tm_in, tms),
         ))
     ]
-    for fetch in fetches:
+    for fetch in fetches[:2]:
         fetch.start()
 
     barrier = pltpu.get_barrier_semaphore()
@@ -97,6 +112,9 @@
 
     lax.fori_loop(1, n, greet_row, 0)
     lax.fori_loop(1, nc, greet_col, 0)
+
+    for fetch in fetches[2:]:
+        fetch.start()
 
     fetches[0].wait()
     x[0] = normalize(zr[0]).reshape(2, tile, channels)
@@ -105,21 +123,6 @@
     for form in range(2):
         for e in range(2):
             scat[c, form, e] = x[form, e, part(c), :]
-
-    for fetch in fetches[2:]:
-        fetch.wait()
-    for form, w in enumerate((ws, we)):
-        wgt[form] = w[:, 3 * channels : 4 * channels].astype(F32).T.astype(BF16)
-
-    def mask_row(t):
-        return tm[pl.ds(t, 1), :].astype(F32)
-
-    def penalty(t):
-        return (mask_row(t) - 1.0) * 1e9
-
-    key_bias = jnp.concatenate([penalty(2 * c), penalty(2 * c + 1)], axis=1)
-    for h in range(heads):
-        bias[0, h] = (bs[h].astype(F32) + key_bias) * LOG2E
 
     pl.semaphore_wait(barrier, n - 1 + nc - 1)
 
@@ -167,26 +170,26 @@
         return q.at[0, rows, part(p)] if form == 0 else kv.at[1, rows, core, part(p)]
 
     def near_twin(form, b):
-        g = group(b)
+        g = group(form, b)
         landed(q.at[0, pl.ds(0, batch), part(0)], ra.at[form, g])
         own = near_piece(form, g, c)
         remote(own, own, sc.at[form], rt.at[form, g], r, twin).start()
 
     def near_levels(form, b, held):
-        g = group(b)
+        g = group(form, b)
         piece_ref = near_piece(form, g, held)
         for d in range(1, deep):
             remote(piece_ref, piece_ref, sc.at[form], rn.at[form, g], r, level(d)).start()
 
     def relay(form, b):
-        landed(near_piece(form, group(b), twin), rt.at[form, group(b)])
+        landed(near_piece(form, group(form, b), twin), rt.at[form, group(form, b)])
         near_levels(form, b, twin)
 
     def send_facing(form):
         remote(x.at[form], across.at[form], sg.at[form], ry.at[form], facing, c).start()
 
     def spread(form, held, row):
-        for k in range(groups):
+        for k in range(groups) if form == 0 else spans:
             to = 4 * lax.rem(block + k, groups) + 2 * lax.rem(chip, 2)
             for e in range(2):
                 dst = kv.at[0, row, e] if form == 0 else q.at[1, row]
@@ -200,44 +203,83 @@
         landed(x.at[form], ry.at[form])
         spread(form, across, facing)
 
+    def forward_copy(form, g):
+        held = kv.at[form, pl.ds(batch * g, batch), core]
+        return remote(held, held, sf.at[form], rf.at[form, g], mate, c)
+
+    def near_landed(form, g):
+        if form == 0:
+            landed(q.at[0, pl.ds(0, nc - 1), pl.ds(0, batch * piece)], rn.at[form, g])
+        elif deep > 1:
+            landed(q.at[0, pl.ds(0, (nc - 2) * batch // nc)], rn.at[form, g])
+
+    def gather_landed(form, g):
+        landed(q.at[0, pl.ds(0, batch)], rg.at[form, g])
+
+    def forward(form, b):
+        (gather_landed if form == 0 else near_landed)(form, group(form, b))
+        forward_copy(form, group(form, b)).start()
+
     lax.fori_loop(1, nc, scatter, 0)
     send_facing(0)
     spread(0, x, r)
+    bias_swap.start()
+
+    for fetch in fetches[2:]:
+        fetch.wait()
+    for form, w in enumerate((ws, we)):
+        wgt[form] = w[:, 3 * channels : 4 * channels].astype(F32).T.astype(BF16)
+
+    key_bias = jnp.concatenate([penalty(2 * c), penalty(2 * c + 1)], axis=1)
+    for h in range(heads):
+        bias[0, h] = (bs[h].astype(F32) + key_bias) * LOG2E
+
     landed(scat.at[pl.ds(0, nc - 1)], rs)
     cross(0)
     spread_facing(0)
     cross(1)
-    bias_swap.start()
     send_facing(1)
 
-    for b in range(groups):
-        near_twin(0, b)
-    for b in range(groups):
-        near_levels(0, b, c)
-        if b:
-            relay(0, b - 1)
-    relay(0, groups - 1)
+    bias_swap.wait_recv()
+    for source, cols_at, t in ((be, mine, r), (be_in, other, mate)):
+        row = penalty(t)
+        for h in range(heads):
+            bias[1, h, :, cols_at] = (source[h].astype(F32).T + row) * LOG2E
+
+
+    def near_direct(b, carry):
+        g = group(0, b)
+        landed(q.at[0, pl.ds(0, batch), part(0)], ra.at[0, g])
+        own = near_piece(0, g, c)
+        for d in range(1, nc):
+            remote(own, own, sc.at[0], rn.at[0, g], r, lax.rem(c + d, nc)).start()
+        return carry
+
+    lax.fori_loop(0, groups, near_direct, 0)
+
+    def forward_rows(b, carry):
+        forward(0, b)
+        return carry
+
+    lax.fori_loop(0, groups, forward_rows, 0)
     spread(1, x, r)
     for b in range(groups):
         near_twin(1, b)
     for b in range(groups):
         near_levels(1, b, c)
 
-    bias_swap.wait_recv()
-    for source, cols_at, t in ((be, mine, r), (be_in, other, mate)):
-        row = penalty(t)
-        for h in range(heads):
-            bias[1, h, :, cols_at] = (source[h].astype(F32).T + row) * LOG2E
-
     scale = depth ** (-0.5) * LOG2E
     lane = lax.broadcasted_iota(jnp.int32, (tile, channels), 1)
     head_of = lane // depth
     ones = jnp.ones((2 * tile, channels), BF16)
 
+    def project(form, w, g):
+        rows = kv[form, pl.ds(batch * g, batch)].reshape(2 * batch * tile, channels)
+        return nn(rows, w[:, channels : 3 * channels]).astype(BF16)
+
     def attend(form, w, g):
         held = pl.ds(batch * g, batch)
-        rows = kv[form, held].reshape(2 * batch * tile, channels)
-        both = nn(rows, w[:, channels : 3 * channels]).astype(BF16)
+        both = projected[g] if form == 0 else project(form, w, g)
         rows = q[form, held].reshape(batch * tile, channels)
         queries = nn(rows, w[:, :channels]) * scale
         for i in range(batch):
@@ -263,57 +305,34 @@
             pn[form, a] = numer.T.astype(BF16)
             pst[form, a] = stats.T[: 2 * heads]
 
-    def forward_copy(form, g):
-        held = kv.at[form, pl.ds(batch * g, batch), core]
-        return remote(held, held, sf.at[form], rf.at[form, g], mate, c)
-
-    def near_landed(form, g):
-        if deep > 1:
-            landed(q.at[0, pl.ds(0, (nc - 2) * batch // nc)], rn.at[form, g])
-
-    def gather_landed(form, g):
-        landed(q.at[0, pl.ds(0, batch)], rg.at[form, g])
-
-    def forward(form, b):
-        (gather_landed if form == 0 else near_landed)(form, group(b))
-        forward_copy(form, group(b)).start()
-
     def send_partial(form, a):
         if form == 0:
-            to, b = a // per, lax.rem(a, per)
-            pairs = (rsn.at[c, b], rsn_sem), (rss.at[c, b], rss_sem)
-            here, row, col = to == c, r, to
+            to, b = lax.rem(a // per, deep), lax.rem(a, per)
+            pairs = (rsn.at[lane_z, b], rsn_sem), (rss.at[lane_z, b], rss_sem)
+            here, row, col = to == lane_z, r, lap * deep + to
         else:
             pairs = (ren.at[core, chip], ren_sem.at[core]), (res.at[core, chip], res_sem.at[core])
             here, row, col = a == r, a, c
         either(here, pn.at[form, a], pairs[0][0], spn.at[form], pairs[0][1], row, col)
         either(here, pst.at[form, a], pairs[1][0], sps.at[form], pairs[1][1], row, col)
 
-    def run_form(form, w):
-        forward(form, 0)
-
-        def step(b, carry):
-            g = group(b)
-            if form == 0:
-                @pl.when(b == 0)
-                def _():
-                    spread_facing(1)
-                relay(1, b)
-            @pl.when(b + 1 < groups)
-            def _():
-                forward(form, b + 1)
-            (near_landed if form == 0 else gather_landed)(form, g)
-            forward_copy(form, g).wait_recv()
-            if form == 1:
-                for k in range(batch):
-                    send_partial(0, batch * g + k)
-            attend(form, w, g)
-            if form == 1:
-                for k in range(batch):
-                    send_partial(1, batch * g + k)
-            return carry
-
-        lax.fori_loop(0, groups, step, 0)
+    def send_twin_partial(g):
+        @pl.when(g // side != lap)
+        def _():
+            rows, slot = pl.ds(batch * g, batch), lax.rem(g, side)
+            remote(pn.at[0, rows], twn.at[slot], spn.at[0], twn_sem.at[slot], r, twin).start()
+            remote(pst.at[0, rows], tws.at[slot], sps.at[0], tws_sem.at[slot], r, twin).start()
+
+    def merge_twin(slot):
+        landed(twn.at[slot], twn_sem.at[slot])
+        landed(tws.at[slot], tws_sem.at[slot])
+        for k in range(batch):
+            a = batch * (lap * side + slot) + k
+            numer, largest, denom = combine([pn[0, a], twn[slot, k]], [pst[0, a], tws[slot, k]])
+            pn[0, a] = jnp.concatenate(numer, axis=0).astype(BF16)
+            pst[0, a, :heads] = largest
+            pst[0, a, heads:] = denom
+            send_partial(0, a)
 
     def combine(parts, stats):
         peaks = [s[:heads] for s in stats]
@@ -323,9 +342,52 @@
         rows = []
         for h in range(heads):
             pick = slice(h * depth, (h + 1) * depth)
-            total = sum(f[h : h + 1] * p[pick].astype(F32) for f, p in zip(factors, parts))
-            rows.append(total / denom[h : h + 1])
-        return jnp.concatenate(rows, axis=0)
+            rows.append(sum(f[h : h + 1] * p[pick].astype(F32) for f, p in zip(factors, parts)))
+        return rows, largest, denom
+
+    def divided(parts, stats):
+        rows, _, denom = combine(parts, stats)
+        return jnp.concatenate([row / denom[h : h + 1] for h, row in enumerate(rows)], axis=0)
+
+    def run_form(form, w):
+        if form == 0:
+            def ahead(b, carry):
+                g = group(0, b)
+                forward_copy(0, g).wait_recv()
+                projected[g] = project(0, w, g)
+                return carry
+
+            lax.fori_loop(0, groups, ahead, 0)
+        else:
+            forward(form, 0)
+
+        def step(b, carry):
+            g = group(form, b)
+            if form == 0:
+                @pl.when(b == 0)
+                def _():
+                    spread_facing(1)
+                relay(1, b)
+            if form == 0:
+                near_landed(form, g)
+            else:
+                @pl.when(b + 1 < groups)
+                def _():
+                    forward(form, b + 1)
+                gather_landed(form, g)
+                forward_copy(form, g).wait_recv()
+            attend(form, w, g)
+            if form == 0:
+                send_twin_partial(g)
+            else:
+                @pl.when((b >= MERGE) & (b < MERGE + groups // 2))
+                def _():
+                    merge_twin(b - MERGE)
+                for k in range(batch):
+                    send_partial(1, batch * g + k)
+            return carry
+
+        lax.fori_loop(0, groups, step, 0)
 
     def finish(form, attended, rows, weight, mask):
         gate = nt(wgt[form], rows)
@@ -343,14 +405,14 @@
     landed(rss, rss_sem)
     for b in range(per):
         a = per * c + b
-        attended = combine([rsn[g, b] for g in range(nc)], [rss[g, b] for g in range(nc)])
+        attended = divided([rsn[g, b] for g in range(deep)], [rss[g, b] for g in range(deep)])
         mask = mask_row(r) * mask_scalar(0, a)
         out_s[b] = finish(0, attended, q[0, a], wso[...], mask)
 
     for e in range(2):
         landed(ren.at[e], ren_sem.at[e])
         landed(res.at[e], res_sem.at[e])
-        attended = combine([ren[e, m] for m in range(nc)], [res[e, m] for m in range(nc)])
+        attended = divided([ren[e, m] for m in range(nc)], [res[e, m] for m in range(nc)])
         mask = mask_row(2 * c + e) * mask_scalar(1, r)
         out_e[0, e * tile : (e + 1) * tile, :] = finish(1, attended, x[1, e], weo[...], mask)
 
@@ -405,13 +467,16 @@
             pltpu.VMEM((heads, tile, tile), BF16),
             pltpu.VMEM((2, n, channels, tile), BF16),
             pltpu.VMEM((2, n, 2 * heads, tile), F32),
-            pltpu.VMEM((nc, per, channels, tile), BF16),
-            pltpu.VMEM((nc, per, 2 * heads, tile), F32),
+            pltpu.VMEM((nc // 2, per, channels, tile), BF16),
+            pltpu.VMEM((nc // 2, per, 2 * heads, tile), F32),
             pltpu.VMEM((2, nc, channels, tile), BF16),
             pltpu.VMEM((2, nc, 2 * heads, tile), F32),
+            pltpu.VMEM((groups // 2, n // groups, channels, tile), BF16),
+            pltpu.VMEM((groups // 2, n // groups, 2 * heads, tile), F32),
+            pltpu.VMEM((groups, n // groups * span, 2 * channels), BF16),
             dma, dma((2,)), dma((2,)), dma((2,)), dma((2,)), dma((2,)), dma((2,)), dma,
             dma, dma((2, groups)), dma((2, groups)), dma((2,)), dma((2, groups)), dma((2, groups)), dma((2, groups)),
-            dma, dma, dma((2,)), dma((2,)), dma,
+            dma, dma, dma((2,)), dma((2,)), dma((groups // 2,)), dma((groups // 2,)), dma,
         ],
         compiler_params=pltpu.CompilerParams(
             collective_id=0, has_side_effects=True, vmem_limit_bytes=62 * 1024 * 1024

time: 53.3 us -> 48.7 us (0.914)
  the two profiles are of different devices: /device:TPU:40 before, /device:TPU:1 now
where the time goes in v5:
time: 48.7 us; the launch traced here: 48.1 us
  Pallas kernels  45.3 us (93%)
  local copies, waits for them, and re-layouts  2.14 us (4%)
  between operations  0.65 us (1%)
    pallas_call x1, Pallas kernels, local(): pl.pallas_call(functools.partial(kernel, n, nc, heads), out_shape=(jax.Sh...  45.3 us
    unnamed x4, local copies, waits for them, and re-layouts  2.14 us

profile of v5, /device:TPU:1, one launch (start us, length us, event | category | flops | bytes accessed | tf_op | source)
XLA Modules:
  0.0 48.1 jit_solution(11258576079648324569)
XLA Ops:
  0.6 45.3 %triangle_attention.1 = (bf16[2,128,128]{2,1,0:T(8,128)(2,1)}, bf16[1,256,128]{2,1,0:T(8,128)(2,1)}) custom-call(bf16[1,256,128]{2,1,0:T(8,128)(2,1)} %zr_in.1, bf16[1,256,128]{2,1,0:T(8,128)(2,1)} %zc_in.1, bf16[4,128,256]{2,1,0:T(8,128)(2,1)} %bs_in.1, bf16[4,128,256]{2,1,0:T(8,128)(2,1)} %be_far.1, bf16[128,512]{1,0:T(8,128)(2,1)} %ws_in.1, ...), custom_call_target="tpu_custom_call" | custom-call | tf_op jit(solution)/shard_map/triangle_attention/pallas_call | solution.py:440
  45.9 0.0 copy-start
  45.9 1.5 %copy.14 = bf16[2,128,128]{2,1,0:T(8,128)(2,1)} copy(bf16[2,128,128]{2,1,0:T(8,128)(2,1)} %get-tuple-element.4) | data formatting | bytes 131072
  47.4 0.0 copy-done
  47.4 0.6 %copy.15 = bf16[1,256,128]{2,1,0:T(8,128)(2,1)} copy(bf16[1,256,128]{2,1,0:T(8,128)(2,1)S(1)} %copy-done) | data formatting | bytes 131072
Async XLA Ops:
  45.9 1.5 %copy-start = (bf16[1,256,128]{2,1,0:T(8,128)(2,1)S(1)}, bf16[1,256,128]{2,1,0:T(8,128)(2,1)}, u32[]{:S(2)}) copy-start(bf16[1,256,128]{2,1,0:T(8,128)(2,1)} %get-tuple-element.5) | copy-start | bytes 196612

commit v6 on v5

--- a/solution.py
+++ b/solution.py
@@ -110,8 +110,10 @@
         greet(r, lax.rem(c + d, nc))
         return carry
 
-    lax.fori_loop(1, n, greet_row, 0)
-    lax.fori_loop(1, nc, greet_col, 0)
+    for d in sorted(range(1, n), key=lambda d: -min(d, n - d)):
+        greet_row(d, 0)
+    for d in sorted(range(1, nc), key=lambda d: -min(d, nc - d)):
+        greet_col(d, 0)
 
     for fetch in fetches[2:]:
         fetch.start()
@@ -209,7 +211,7 @@
 
     def near_landed(form, g):
         if form == 0:
-            landed(q.at[0, pl.ds(0, nc - 1), pl.ds(0, batch * piece)], rn.at[form, g])
+            landed(q.at[0, pl.ds(0, batch // 2)], rn.at[form, g])
         elif deep > 1:
             landed(q.at[0, pl.ds(0, (nc - 2) * batch // nc)], rn.at[form, g])
 
@@ -236,37 +238,41 @@
 
     landed(scat.at[pl.ds(0, nc - 1)], rs)
     cross(0)
+    cross(1)
     spread_facing(0)
-    cross(1)
     send_facing(1)
 
-    bias_swap.wait_recv()
-    for source, cols_at, t in ((be, mine, r), (be_in, other, mate)):
-        row = penalty(t)
-        for h in range(heads):
-            bias[1, h, :, cols_at] = (source[h].astype(F32).T + row) * LOG2E
-
-
-    def near_direct(b, carry):
+    def near_level(b, carry):
         g = group(0, b)
         landed(q.at[0, pl.ds(0, batch), part(0)], ra.at[0, g])
         own = near_piece(0, g, c)
-        for d in range(1, nc):
-            remote(own, own, sc.at[0], rn.at[0, g], r, lax.rem(c + d, nc)).start()
+        for d in range(1, deep):
+            remote(own, own, sc.at[0], rt.at[0, g], r, level(d)).start()
+        remote(own, own, sc.at[0], rn.at[0, g], r, twin).start()
         return carry
 
-    lax.fori_loop(0, groups, near_direct, 0)
+    def level_to_twin(b):
+        g = group(0, b)
+        landed(q.at[0, pl.ds(0, (deep - 1) * batch), part(0)], rt.at[0, g])
+        for d in range(1, deep):
+            held = near_piece(0, g, level(d))
+            remote(held, held, sc.at[0], rn.at[0, g], r, twin).start()
 
     def forward_rows(b, carry):
         forward(0, b)
         return carry
 
+    lax.fori_loop(0, groups, near_level, 0)
     lax.fori_loop(0, groups, forward_rows, 0)
-    spread(1, x, r)
     for b in range(groups):
         near_twin(1, b)
     for b in range(groups):
         near_levels(1, b, c)
+    level_to_twin(0)
+    level_to_twin(1)
+    level_to_twin(2)
+    level_to_twin(3)
+    spread(1, x, r)
 
     scale = depth ** (-0.5) * LOG2E
     lane = lax.broadcasted_iota(jnp.int32, (tile, channels), 1)
@@ -380,11 +386,11 @@
             if form == 0:
                 send_twin_partial(g)
             else:
+                for k in range(batch):
+                    send_partial(1, batch * g + k)
                 @pl.when((b >= MERGE) & (b < MERGE + groups // 2))
                 def _():
                     merge_twin(b - MERGE)
-                for k in range(batch):
-                    send_partial(1, batch * g + k)
             return carry
 
         lax.fori_loop(0, groups, step, 0)
@@ -395,6 +401,13 @@
         return nn(gated.T.astype(BF16), weight).astype(BF16)
 
     run_form(0, ws)
+    bias_swap.wait_recv()
+    for source, cols_at, t in ((be, mine, r), (be_in, other, mate)):
+        row = penalty(t)
+        for h in range(heads):
+            bias[1, h, :, cols_at] = (source[h].astype(F32).T + row) * LOG2E
+
+
     run_form(1, we)
 
     def mask_scalar(k, a):

time: 48.7 us -> 47.9 us (0.984)
  Pallas kernels: 45.3 us -> 44.6 us
    pallas_call x1, Pallas kernels: 45.3 us -> 44.6 us  [local(): pl.pallas_call(functools.partial(kernel, n, nc, heads), out_shape=(jax.Sh...]
where the time goes in v6:
time: 47.9 us; the launch traced here: 47.4 us
  Pallas kernels  44.6 us (93%)
  local copies, waits for them, and re-layouts  2.14 us (4%)
  between operations  0.65 us (1%)
    pallas_call x1, Pallas kernels, local(): pl.pallas_call(functools.partial(kernel, n, nc, heads), out_shape=(jax.Sh...  44.6 us
    unnamed x4, local copies, waits for them, and re-layouts  2.14 us

profile of v6, /device:TPU:1, one launch (start us, length us, event | category | flops | bytes accessed | tf_op | source)
XLA Modules:
  0.0 47.4 jit_solution(15434134218172865110)
XLA Ops:
  0.6 44.6 %triangle_attention.1 = (bf16[2,128,128]{2,1,0:T(8,128)(2,1)}, bf16[1,256,128]{2,1,0:T(8,128)(2,1)}) custom-call(bf16[1,256,128]{2,1,0:T(8,128)(2,1)} %zr_in.1, bf16[1,256,128]{2,1,0:T(8,128)(2,1)} %zc_in.1, bf16[4,128,256]{2,1,0:T(8,128)(2,1)} %bs_in.1, bf16[4,128,256]{2,1,0:T(8,128)(2,1)} %be_far.1, bf16[128,512]{1,0:T(8,128)(2,1)} %ws_in.1, ...), custom_call_target="tpu_custom_call" | custom-call | tf_op jit(solution)/shard_map/triangle_attention/pallas_call | solution.py:453
  45.2 0.0 copy-start
  45.2 1.5 %copy.14 = bf16[2,128,128]{2,1,0:T(8,128)(2,1)} copy(bf16[2,128,128]{2,1,0:T(8,128)(2,1)} %get-tuple-element.4) | data formatting | bytes 131072
  46.7 0.0 copy-done
  46.7 0.6 %copy.15 = bf16[1,256,128]{2,1,0:T(8,128)(2,1)} copy(bf16[1,256,128]{2,1,0:T(8,128)(2,1)S(1)} %copy-done) | data formatting | bytes 131072
Async XLA Ops:
  45.2 1.5 %copy-start = (bf16[1,256,128]{2,1,0:T(8,128)(2,1)S(1)}, bf16[1,256,128]{2,1,0:T(8,128)(2,1)}, u32[]{:S(2)}) copy-start(bf16[1,256,128]{2,1,0:T(8,128)(2,1)} %get-tuple-element.5) | copy-start | bytes 196612

commit v7 on v6

--- a/solution.py
+++ b/solution.py
@@ -268,11 +268,6 @@
         near_twin(1, b)
     for b in range(groups):
         near_levels(1, b, c)
-    level_to_twin(0)
-    level_to_twin(1)
-    level_to_twin(2)
-    level_to_twin(3)
-    spread(1, x, r)
 
     scale = depth ** (-0.5) * LOG2E
     lane = lax.broadcasted_iota(jnp.int32, (tile, channels), 1)
@@ -363,7 +358,15 @@
                 projected[g] = project(0, w, g)
                 return carry
 
-            lax.fori_loop(0, groups, ahead, 0)
+            level_to_twin(0)
+            ahead(0, 0)
+            level_to_twin(1)
+            ahead(1, 0)
+            level_to_twin(2)
+            ahead(2, 0)
+            level_to_twin(3)
+            ahead(3, 0)
+            spread(1, x, r)
         else:
             forward(form, 0)
 
@@ -395,9 +398,11 @@
 
         lax.fori_loop(0, groups, step, 0)
 
-    def finish(form, attended, rows, weight, mask):
-        gate = nt(wgt[form], rows)
-        gated = jax.nn.sigmoid(gate) * attended * mask
+    def gate(form, rows, mask):
+        return jax.nn.sigmoid(nt(wgt[form], rows)) * mask
+
+    def finish(gates, attended, weight):
+        gated = gates * attended
         return nn(gated.T.astype(BF16), weight).astype(BF16)
 
     run_form(0, ws)
@@ -414,20 +419,19 @@
         at = offs[k] + a
         return tms[at // tile, lax.rem(at, tile)].astype(F32)
 
+    gates_s = [gate(0, q[0, per * c + b], mask_row(r) * mask_scalar(0, per * c + b)) for b in range(per)]
+    gates_e = [gate(1, x[1, e], mask_row(2 * c + e) * mask_scalar(1, r)) for e in range(2)]
     landed(rsn, rsn_sem)
     landed(rss, rss_sem)
     for b in range(per):
-        a = per * c + b
         attended = divided([rsn[g, b] for g in range(deep)], [rss[g, b] for g in range(deep)])
-        mask = mask_row(r) * mask_scalar(0, a)
-        out_s[b] = finish(0, attended, q[0, a], wso[...], mask)
+        out_s[b] = finish(gates_s[b], attended, wso[...])
 
     for e in range(2):
         landed(ren.at[e], ren_sem.at[e])
         landed(res.at[e], res_sem.at[e])
         attended = divided([ren[e, m] for m in range(nc)], [res[e, m] for m in range(nc)])
-        mask = mask_row(2 * c + e) * mask_scalar(1, r)
-        out_e[0, e * tile : (e + 1) * tile, :] = finish(1, attended, x[1, e], weo[...], mask)
+        out_e[0, e * tile : (e + 1) * tile, :] = finish(gates_e[e], attended, weo[...])
 
     bias_swap.wait_send()
     gone(scat.at[pl.ds(0, nc - 1)], ss)

time: 47.9 us -> 47.3 us (0.987)
  no operation moved by 1% of the time
where the time goes in v7:
time: 47.3 us; the launch traced here: 47.1 us
  Pallas kernels  44.3 us (94%)
  local copies, waits for them, and re-layouts  2.14 us (5%)
  between operations  0.65 us (1%)
    pallas_call x1, Pallas kernels, local(): pl.pallas_call(functools.partial(kernel, n, nc, heads), out_shape=(jax.Sh...  44.3 us
    unnamed x4, local copies, waits for them, and re-layouts  2.14 us

profile of v7, /device:TPU:1, one launch (start us, length us, event | category | flops | bytes accessed | tf_op | source)
XLA Modules:
  0.0 47.1 jit_solution(2382360486196537601)
XLA Ops:
  0.6 44.3 %triangle_attention.1 = (bf16[2,128,128]{2,1,0:T(8,128)(2,1)}, bf16[1,256,128]{2,1,0:T(8,128)(2,1)}) custom-call(bf16[1,256,128]{2,1,0:T(8,128)(2,1)} %zr_in.1, bf16[1,256,128]{2,1,0:T(8,128)(2,1)} %zc_in.1, bf16[4,128,256]{2,1,0:T(8,128)(2,1)} %bs_in.1, bf16[4,128,256]{2,1,0:T(8,128)(2,1)} %be_far.1, bf16[128,512]{1,0:T(8,128)(2,1)} %ws_in.1, ...), custom_call_target="tpu_custom_call" | custom-call | tf_op jit(solution)/shard_map/triangle_attention/pallas_call | solution.py:457
  45.0 0.0 copy-start
  45.0 1.5 %copy.14 = bf16[2,128,128]{2,1,0:T(8,128)(2,1)} copy(bf16[2,128,128]{2,1,0:T(8,128)(2,1)} %get-tuple-element.4) | data formatting | bytes 131072
  46.5 0.0 copy-done
  46.5 0.6 %copy.15 = bf16[1,256,128]{2,1,0:T(8,128)(2,1)} copy(bf16[1,256,128]{2,1,0:T(8,128)(2,1)S(1)} %copy-done) | data formatting | bytes 131072
Async XLA Ops:
  45.0 1.5 %copy-start = (bf16[1,256,128]{2,1,0:T(8,128)(2,1)S(1)}, bf16[1,256,128]{2,1,0:T(8,128)(2,1)}, u32[]{:S(2)}) copy-start(bf16[1,256,128]{2,1,0:T(8,128)(2,1)} %get-tuple-element.5) | copy-start | bytes 196612

commit v8 on v7

--- a/solution.py
+++ b/solution.py
@@ -350,6 +350,13 @@
         rows, _, denom = combine(parts, stats)
         return jnp.concatenate([row / denom[h : h + 1] for h, row in enumerate(rows)], axis=0)
 
+    def prepare_ending_bias():
+        bias_swap.wait_recv()
+        for source, cols_at, t in ((be, mine, r), (be_in, other, mate)):
+            row = penalty(t)
+            for h in range(heads):
+                bias[1, h, :, cols_at] = (source[h].astype(F32).T + row) * LOG2E
+
     def run_form(form, w):
         if form == 0:
             def ahead(b, carry):
@@ -367,6 +374,7 @@
             level_to_twin(3)
             ahead(3, 0)
             spread(1, x, r)
+            prepare_ending_bias()
         else:
             forward(form, 0)
 
@@ -389,8 +397,16 @@
             if form == 0:
                 send_twin_partial(g)
             else:
-                for k in range(batch):
-                    send_partial(1, batch * g + k)
+                @pl.when(b + 1 < groups)
+                def _():
+                    for k in range(batch):
+                        a = batch * g + k
+                        remote(pn.at[1, a], ren.at[core, chip], spn.at[1], ren_sem.at[core], a, c).start()
+                        remote(pst.at[1, a], res.at[core, chip], sps.at[1], res_sem.at[core], a, c).start()
+                @pl.when(b + 1 == groups)
+                def _():
+                    for k in range(batch):
+                        send_partial(1, batch * g + k)
                 @pl.when((b >= MERGE) & (b < MERGE + groups // 2))
                 def _():
                     merge_twin(b - MERGE)
@@ -406,13 +422,6 @@
         return nn(gated.T.astype(BF16), weight).astype(BF16)
 
     run_form(0, ws)
-    bias_swap.wait_recv()
-    for source, cols_at, t in ((be, mine, r), (be_in, other, mate)):
-        row = penalty(t)
-        for h in range(heads):
-            bias[1, h, :, cols_at] = (source[h].astype(F32).T + row) * LOG2E
-
-
     run_form(1, we)
 
     def mask_scalar(k, a):

time: 47.3 us -> 47.3 us (level)
  no operation moved by 1% of the time
where the time goes in v8:
time: 47.3 us; the launch traced here: 47.1 us
  Pallas kernels  44.3 us (94%)
  local copies, waits for them, and re-layouts  2.14 us (5%)
  between operations  0.65 us (1%)
    pallas_call x1, Pallas kernels, local(): pl.pallas_call(functools.partial(kernel, n, nc, heads), out_shape=(jax.Sh...  44.3 us
    unnamed x4, local copies, waits for them, and re-layouts  2.14 us

profile of v8, /device:TPU:1, one launch (start us, length us, event | category | flops | bytes accessed | tf_op | source)
XLA Modules:
  0.0 47.1 jit_solution(4274376681034476158)
XLA Ops:
  0.6 44.3 %triangle_attention.1 = (bf16[2,128,128]{2,1,0:T(8,128)(2,1)}, bf16[1,256,128]{2,1,0:T(8,128)(2,1)}) custom-call(bf16[1,256,128]{2,1,0:T(8,128)(2,1)} %zr_in.1, bf16[1,256,128]{2,1,0:T(8,128)(2,1)} %zc_in.1, bf16[4,128,256]{2,1,0:T(8,128)(2,1)} %bs_in.1, bf16[4,128,256]{2,1,0:T(8,128)(2,1)} %be_far.1, bf16[128,512]{1,0:T(8,128)(2,1)} %ws_in.1, ...), custom_call_target="tpu_custom_call" | custom-call | tf_op jit(solution)/shard_map/triangle_attention/pallas_call | solution.py:466
  44.9 0.0 copy-start
  45.0 1.5 %copy.14 = bf16[2,128,128]{2,1,0:T(8,128)(2,1)} copy(bf16[2,128,128]{2,1,0:T(8,128)(2,1)} %get-tuple-element.4) | data formatting | bytes 131072
  46.5 0.0 copy-done
  46.5 0.6 %copy.15 = bf16[1,256,128]{2,1,0:T(8,128)(2,1)} copy(bf16[1,256,128]{2,1,0:T(8,128)(2,1)S(1)} %copy-done) | data formatting | bytes 131072
Async XLA Ops:
  44.9 1.5 %copy-start = (bf16[1,256,128]{2,1,0:T(8,128)(2,1)S(1)}, bf16[1,256,128]{2,1,0:T(8,128)(2,1)}, u32[]{:S(2)}) copy-start(bf16[1,256,128]{2,1,0:T(8,128)(2,1)} %get-tuple-element.5) | copy-start | bytes 196612

commit v9 on v7

--- a/solution.py
+++ b/solution.py
@@ -373,10 +373,10 @@
         def step(b, carry):
             g = group(form, b)
             if form == 0:
-                @pl.when(b == 0)
+                relay(1, b)
+                @pl.when(b == 1)
                 def _():
                     spread_facing(1)
-                relay(1, b)
             if form == 0:
                 near_landed(form, g)
             else:

time: 47.3 us -> 47.4 us (level)
  no operation moved by 1% of the time
where the time goes in v9:
time: 47.4 us; the launch traced here: 47.2 us
  Pallas kernels  44.4 us (94%)
  local copies, waits for them, and re-layouts  2.14 us (5%)
  between operations  0.65 us (1%)
    pallas_call x1, Pallas kernels, local(): pl.pallas_call(functools.partial(kernel, n, nc, heads), out_shape=(jax.Sh...  44.4 us
    unnamed x4, local copies, waits for them, and re-layouts  2.14 us

profile of v9, /device:TPU:1, one launch (start us, length us, event | category | flops | bytes accessed | tf_op | source)
XLA Modules:
  0.0 47.2 jit_solution(5465687766136168335)
XLA Ops:
  0.6 44.4 %triangle_attention.1 = (bf16[2,128,128]{2,1,0:T(8,128)(2,1)}, bf16[1,256,128]{2,1,0:T(8,128)(2,1)}) custom-call(bf16[1,256,128]{2,1,0:T(8,128)(2,1)} %zr_in.1, bf16[1,256,128]{2,1,0:T(8,128)(2,1)} %zc_in.1, bf16[4,128,256]{2,1,0:T(8,128)(2,1)} %bs_in.1, bf16[4,128,256]{2,1,0:T(8,128)(2,1)} %be_far.1, bf16[128,512]{1,0:T(8,128)(2,1)} %ws_in.1, ...), custom_call_target="tpu_custom_call" | custom-call | tf_op jit(solution)/shard_map/triangle_attention/pallas_call | solution.py:457
  45.1 0.0 copy-start
  45.1 1.5 %copy.14 = bf16[2,128,128]{2,1,0:T(8,128)(2,1)} copy(bf16[2,128,128]{2,1,0:T(8,128)(2,1)} %get-tuple-element.4) | data formatting | bytes 131072
  46.6 0.0 copy-done
  46.6 0.6 %copy.15 = bf16[1,256,128]{2,1,0:T(8,128)(2,1)} copy(bf16[1,256,128]{2,1,0:T(8,128)(2,1)S(1)} %copy-done) | data formatting | bytes 131072
Async XLA Ops:
  45.1 1.5 %copy-start = (bf16[1,256,128]{2,1,0:T(8,128)(2,1)S(1)}, bf16[1,256,128]{2,1,0:T(8,128)(2,1)}, u32[]{:S(2)}) copy-start(bf16[1,256,128]{2,1,0:T(8,128)(2,1)} %get-tuple-element.5) | copy-start | bytes 196612
